TPU v7x, 256 devices: a whole 4x4x8 slice. The times are simulated.
256 devices in a mesh: samp: 64 (over z, y_lo, x), chan: 4 (over y_hi, core).
Axes of the slice: x: 4, y: 4 (y_hi: 2, y_lo: 2; y = y_hi * 2 + y_lo), z: 8, core: 2. Of those that a mesh axis runs over, the one named last changes fastest.
Arguments:
- activations: bfloat16 [50176, 768], P('samp', 'chan'), may hold values from -16 to 16
- gradients: bfloat16 [50176, 3072], P('samp', 'chan'), may hold values from -16 to 16
- basis_act: bfloat16 [768, 768], P(None, 'chan'), may hold values from -0.21875 to 0.21875
- basis_grad: bfloat16 [3072, 3072], P(None, 'chan'), may hold values from -0.109375 to 0.109375
Outputs:
- act_factor: float32 [768, 768], P('samp', 'chan')
- grad_factor: float32 [3072, 3072], P('samp', 'chan')
- eigen_scales: float32 [3072, 768], P('samp', 'chan')
All inputs are finite; a program needn't handle non-finite values.
Results may differ from a plain program's by a relative error of at most 0.0011.
Values may be sent and summed in bfloat16 or wider, within the bound.
No kernel may reach another device: no remote copies, remote signals or barrier semaphores. Data moves between devices by JAX's collectives and lax.ppermute only.
A program may use at most 128 MiB of HBM per device.

v0:
```python
import jax
import jax.numpy as jnp
from jax import lax
from jax.sharding import PartitionSpec as P

HW = 784


def crossed(left, right):
    return lax.dot_general(
        left, right, (((0,), (0,)), ((), ())), preferred_element_type=jnp.float32
    )


def on_device(activations, gradients, basis_act, basis_grad):
    samples = lax.axis_size("samp")
    rows_dev = activations.shape[0]
    images_dev = rows_dev // HW
    inverse = 1.0 / (rows_dev * samples)
    full_act = lax.all_gather(activations, "chan", axis=1, tiled=True)
    full_grad = lax.all_gather(gradients, "chan", axis=1, tiled=True)
    summed = lax.psum(crossed(full_act, activations) * inverse, "samp")
    height = summed.shape[0] // samples
    act_factor = lax.dynamic_slice_in_dim(summed, lax.axis_index("samp") * height, height, 0)
    partial_grad = crossed(gradients, full_grad) * inverse
    grad_factor = lax.psum_scatter(partial_grad, "samp", scatter_dimension=1, tiled=True).T
    proj_act = jnp.dot(full_act, basis_act, preferred_element_type=jnp.float32).astype(jnp.bfloat16)
    proj_grad = jnp.dot(full_grad, basis_grad, preferred_element_type=jnp.float32).astype(
        jnp.bfloat16
    )
    whole_proj = lax.all_gather(proj_grad, "chan", axis=1, tiled=True)
    act_images = proj_act.reshape(images_dev, HW, proj_act.shape[1])
    weight_all = 1.0 / (images_dev * samples * HW)
    window = whole_proj.reshape(
        images_dev, HW, lax.axis_size("samp") * (whole_proj.shape[1] // samples)
    )
    per_image = jnp.einsum("npf,npc->nfc", window, act_images, preferred_element_type=jnp.float32)
    eigen_scales = lax.psum_scatter(
        jnp.sum(per_image * per_image, axis=0) * weight_all, "samp", scatter_dimension=0, tiled=True
    )
    return (act_factor, grad_factor, eigen_scales)


def solution(mesh):
    return jax.shard_map(
        on_device,
        mesh=mesh,
        in_specs=(P("samp", "chan"), P("samp", "chan"), P(None, "chan"), P(None, "chan")),
        out_specs=(P("samp", "chan"), P("samp", "chan"), P("samp", "chan")),
        check_vma=False,
    )
```

profile of v0, /device:TPU:26, one launch (start us, length us, event | category | flops | bytes accessed | tf_op | source)
XLA Modules:
  0.0 1360.6 jit_solution(11461441748635851487)
XLA Ops:
  7.2 0.0 copy-start
  7.2 0.0 all-gather.6.cloned.1.call-start
  7.2 0.7 all-gather.6.cloned.1.call-update
  7.9 0.0 all-gather.4.cloned.1.call-start
  8.0 0.7 all-gather.4.cloned.1.call-update
  8.7 0.0 copy-start.1
  8.7 0.0 all-gather.8.cloned.1.call-start
  8.7 46.9 %all-gather.6.cloned.1.call-done = bf16[784,3072]{1,0:T(8,128)(2,1)} async-done(((bf16[784,768]{1,0:T(8,128)(2,1)}), bf16[784,3072]{1,0:T(8,128)(2,1)}) %all-gather.6.cloned.1.call-update) | async-done | bytes 4816912 | tf_op jit(solution)/shard_map/all_gather | solution.py:21
  55.6 8.7 convolution_convert_fusion
  64.3 0.0 all-gather.8.cloned.1.call-update
  64.3 0.0 all-reduce.2.cloned.1.call-start
  64.4 17.6 %all-gather.4.cloned.1.call-done = bf16[784,768]{0,1:T(8,128)(2,1)} async-done(((bf16[784,192]{0,1:T(8,128)(2,1)}), bf16[784,768]{0,1:T(8,128)(2,1)}) %all-gather.4.cloned.1.call-update) | async-done | bytes 1204240 | tf_op jit(solution)/shard_map/all_gather | solution.py:20
  82.0 0.0 copy-done.1
  82.0 0.0 copy-start.2
  82.0 2.9 convolution_multiply_fusion.2
  85.0 0.0 all-reduce.2.cloned.1.call-update
  85.0 0.0 reduce-scatter.5.cloned.1.call-start
  85.0 42.9 %all-gather.8.cloned.1.call-done = bf16[784,3072]{1,0:T(8,128)(2,1)} async-done(((bf16[784,768]{1,0:T(8,128)(2,1)}), bf16[784,3072]{1,0:T(8,128)(2,1)}) %all-gather.8.cloned.1.call-update) | async-done | bytes 4816912 | tf_op jit(solution)/shard_map/all_gather | solution.py:31
  127.9 0.0 copy-done
  127.9 0.0 copy-done.2
  127.9 6.8 fusion
  134.8 0.0 copy-start.3
  134.8 0.0 reduce-scatter.5.cloned.1.call-update
  134.8 0.0 reduce-scatter.3.cloned.1.call-start
  134.8 1.2 copy-done.3
  136.0 11.2 convolution_multiply_fusion
  147.3 0.0 reduce-scatter.3.cloned.1.call-update
  147.3 561.8 %all-reduce.2.cloned.1.call-done = f32[768,192]{1,0:T(8,128)} async-done(((f32[768,192]{1,0:T(8,128)}), f32[768,192]{1,0:T(8,128)}) %all-reduce.2.cloned.1.call-update) | async-done | bytes 589840 | tf_op jit(solution)/shard_map/psum | solution.py:22
  709.1 1.3 constant_dynamic-slice_fusion
  710.4 310.4 %reduce-scatter.5.cloned.1.call-done = f32[48,192]{1,0:T(8,128)} async-done(((f32[3072,192]{1,0:T(8,128)}), f32[48,192]{1,0:T(8,128)}) %reduce-scatter.5.cloned.1.call-update) | async-done | bytes 36880 | tf_op jit(solution)/shard_map/reduce_scatter | solution.py:38
  1020.8 333.0 %reduce-scatter.3.cloned.1.call-done = f32[768,48]{0,1:T(8,128)} async-done(((f32[768,3072]{0,1:T(8,128)}), f32[768,48]{0,1:T(8,128)}) %reduce-scatter.3.cloned.1.call-update) | async-done | bytes 147472 | tf_op jit(solution)/shard_map/reduce_scatter | solution.py:26
Async XLA Ops:
  7.2 120.8 %copy-start = (bf16[768,192]{0,1:T(8,128)(2,1)S(1)}, bf16[768,192]{0,1:T(8,128)(2,1)}, u32[]{:S(2)}) copy-start(bf16[768,192]{0,1:T(8,128)(2,1)} %param.6) | copy-start | bytes 884740
  7.2 48.4 %all-gather.6.cloned.1.call-start = ((), (), s32[]{:S(2)}) async-start(), calls=%async_computation.4 | async-start | bytes 6021120 | tf_op jit(solution)/shard_map/all_gather | solution.py:21
  7.9 74.1 %all-gather.4.cloned.1.call-start = ((), (), s32[]{:S(2)}) async-start(), calls=%async_computation.2 | async-start | bytes 1720320 | tf_op jit(solution)/shard_map/all_gather | solution.py:20
  8.7 73.4 %copy-start.1 = (bf16[784,192]{0,1:T(8,128)(2,1)S(1)}, bf16[784,192]{0,1:T(8,128)(2,1)}, u32[]{:S(2)}) copy-start(bf16[784,192]{0,1:T(8,128)(2,1)} %param.4) | copy-start | bytes 903172
  8.7 119.3 %all-gather.8.cloned.1.call-start = ((), (), s32[]{:S(2)}) async-start(), calls=%async_computation.6 | async-start | bytes 6021120 | tf_op jit(solution)/shard_map/all_gather | solution.py:31
  64.3 644.7 %all-reduce.2.cloned.1.call-start = ((), (), s32[]{:S(2)}) async-start(), calls=%async_computation.3 | async-start | bytes 1572864 | tf_op jit(solution)/shard_map/psum | solution.py:22
  82.0 45.9 %copy-start.2 = (bf16[784,768]{0,1:T(8,128)(2,1)S(1)}, bf16[784,768]{0,1:T(8,128)(2,1)}, u32[]{:S(2)}) copy-start(bf16[784,768]{0,1:T(8,128)(2,1)} %all-gather.4.cloned.1.call-done) | copy-start | bytes 3612676
  85.0 935.8 %reduce-scatter.5.cloned.1.call-start = ((), (), s32[]{:S(2)}) async-start(), calls=%async_computation.7 | async-start | bytes 3194880 | tf_op jit(solution)/shard_map/reduce_scatter | solution.py:38
  134.8 1.3 copy-start.3
  134.8 1219.0 %reduce-scatter.3.cloned.1.call-start = ((), (), s32[]{:S(2)}) async-start(), calls=%async_computation.5 | async-start | bytes 9584640 | tf_op jit(solution)/shard_map/reduce_scatter | solution.py:26
Sparse Core Ops, SparseCore 0:
  9.8 45.7 all-gather.5
  57.4 24.5 all-gather.3
  83.8 44.0 all-gather.7
  130.4 578.5 all-reduce.1
  712.1 308.5 reduce-scatter.4
  1023.7 330.0 reduce-scatter.2
where the time goes:
time: 1370 us; the launch traced here: 1360 us
  waiting for transfers between devices  1310 us (96%)
  matrix products  29.7 us (2%)
  between operations  14.1 us (1%)
    psum x1, waiting for transfers between devices, on_device(): summed = lax.psum(crossed(full_act, activations) * inverse, 'samp')  562 us
    reduce_scatter x1, waiting for transfers between devices, on_device(): lax.psum_scatter(partial_grad, 'samp', scatter_dimension=1, tiled=True)  333 us
    reduce_scatter x1, waiting for transfers between devices, on_device(): lax.psum_scatter(jnp.sum(per_image * per_image, axis=0) * weight_all, 'sa...  310 us
    all_gather x1, waiting for transfers between devices, on_device(): full_grad = lax.all_gather(gradients, 'chan', axis=1, tiled=True)  46.9 us
    all_gather x1, waiting for transfers between devices, on_device(): whole_proj = lax.all_gather(proj_grad, 'chan', axis=1, tiled=True)  42.9 us
  transfers between devices with their start and end apart: 6, of which 6 were waited for; matrix products, arithmetic and copies ran while one was open for 2% of the time, Pallas kernels for 0%

commit v1 on v0

v1 whole, which is shorter than its diff:
```python
import functools

import jax
import jax.numpy as jnp
from jax import lax
from jax.experimental import pallas as pl
from jax.experimental.pallas import tpu as pltpu
from jax.sharding import Mesh, PartitionSpec as P

AXES = ("z", "yl", "x", "yh", "core")
SIZES = (8, 2, 4, 2, 2)
SAMP = ("z", "yl", "x")
CHAN = ("yh", "core")
HW = 784
ROWS = 50176
BLOCK = 768
TILE = 48
HALF = 24
PAD = 16
QUARTER = 192
f32, bf16 = jnp.float32, jnp.bfloat16
VMEM = pl.BlockSpec(memory_space=pltpu.VMEM)
SMEM = pl.BlockSpec(memory_space=pltpu.SMEM)
PARAMS = pltpu.CompilerParams(vmem_limit_bytes=48 << 20)


def crossed(left, right):
    return lax.dot_general(
        left, right, (((0,), (0,)), ((), ())), preferred_element_type=f32
    )


def exponent_of(peak):
    e = jnp.floor(jnp.log2(jnp.maximum(peak, 1e-30))) + 1.0
    return jnp.clip(e, -100.0, 100.0)


def coded(value):
    second = value * value
    fourth = second * second
    eighth = fourth * fourth
    return jnp.where(value < 0, -eighth, eighth)


def decoded(code):
    wide = code.astype(f32)
    root = jnp.exp(0.125 * jnp.log(jnp.maximum(jnp.abs(wide), 1e-37)))
    return jnp.where(wide < 0, -root, root)


def scale_of(e):
    return jnp.exp2(14.0 - e)


def unscale_of(rows):
    return jnp.exp2(rows[0:1, 0:1].astype(f32) - 14.0)


def peak_of(value, peak):
    return jnp.maximum(peak, jnp.max(jnp.abs(value), axis=(0, 1), keepdims=True))


def spread(e, rows, width):
    return jnp.broadcast_to(e, (rows, width))


def call(kernel, name, out_shape, in_specs, scratch=(), flops=0, size=0):
    return pl.pallas_call(
        kernel,
        out_shape=out_shape,
        in_specs=in_specs,
        out_specs=jax.tree.map(lambda _: VMEM, out_shape),
        scratch_shapes=list(scratch),
        compiler_params=PARAMS,
        cost_estimate=pl.CostEstimate(flops=1, bytes_accessed=1, transcendentals=0),
        name=name,
    )


def shape(rows, columns=BLOCK, dtype=bf16):
    return jax.ShapeDtypeStruct((rows, columns), dtype)


def factor_kernel(idx, own, same, other, o0, o1, o2, o3, p):
    x, core = idx[2], idx[4]
    peak = jnp.zeros((1, 1), f32)
    for b, rows in enumerate((same, other)):
        for c in range(3):
            cols = slice(c * 256, (c + 1) * 256)
            tile = crossed(rows[...], own[:, cols]) * (1.0 / ROWS)
            p[b, :, cols] = tile
            peak = peak_of(tile, peak)
    e = exponent_of(peak)
    scale = scale_of(e)
    for d, out in enumerate((o0, o1, o2, o3)):
        to = lax.rem(x + d, 4)
        for b, slot in enumerate((core, 1 - core)):
            for hy in range(4):
                src = pl.multiple_of((hy * 4 + to) * TILE, TILE)
                dst = pl.multiple_of((slot * 4 + hy) * TILE, TILE)
                out[pl.ds(dst, TILE), :] = coded(p[b, pl.ds(src, TILE), :] * scale).astype(bf16)
        out[8 * TILE :, :] = spread(e, PAD, BLOCK).astype(bf16)


def factor_messages(idx, own, same, other):
    return call(
        factor_kernel,
        "factor",
        [shape(8 * TILE + PAD)] * 4,
        [SMEM] + [VMEM] * 3,
        [pltpu.VMEM((2, BLOCK, BLOCK), f32)],
    )(idx, own, same, other)


def factor_sum_x_kernel(idx, m0, m1, m2, m3, send, keep, held):
    yl = idx[1]
    factors = [unscale_of(m[8 * TILE :, 0:128]) for m in (m0, m1, m2, m3)]

    def total(b, y):
        rows = pl.ds(pl.multiple_of((b * 2 + y) * TILE, TILE), TILE)
        parts = [decoded(m[rows, :]) * u for m, u in zip((m0, m1, m2, m3), factors)]
        return (parts[0] + parts[1]) + (parts[2] + parts[3])

    peak = jnp.zeros((1, 1), f32)
    for b in range(4):
        keep[b * TILE : (b + 1) * TILE, :] = total(b, yl)
        out = total(b, 1 - yl)
        held[b * TILE : (b + 1) * TILE, :] = out
        peak = peak_of(out, peak)
    e = exponent_of(peak)
    send[0 : 4 * TILE, :] = coded(held[...] * scale_of(e)).astype(bf16)
    send[4 * TILE :, :] = spread(e, PAD, BLOCK).astype(bf16)


def factor_sum_x(idx, messages):
    return call(
        factor_sum_x_kernel,
        "factor_sum_x",
        [shape(4 * TILE + PAD), shape(4 * TILE, dtype=f32)],
        [SMEM] + [VMEM] * 4,
        [pltpu.VMEM((4 * TILE, BLOCK), f32)],
    )(idx, *messages)


def factor_sum_y_kernel(idx, keep_a, got_a, keep_b, got_b, out, held):
    yh = idx[3]
    peak = jnp.zeros((1, 1), f32)
    for keep, got, half in ((keep_a, got_a, yh), (keep_b, got_b, 1 - yh)):
        unscale = unscale_of(got[4 * TILE :, 0:128])
        for b in range(4):
            rows = slice(b * TILE, (b + 1) * TILE)
            tile = keep[rows, :] + decoded(got[rows, :]) * unscale
            held[half * 4 + b] = tile
            peak = peak_of(tile, peak)
    e = exponent_of(peak)
    scale = scale_of(e)
    for z in range(8):
        out[z, 0:TILE, :] = coded(held[z] * scale).astype(bf16)
        out[z, TILE:, :] = spread(e, PAD, BLOCK).astype(bf16)


def factor_sum_y(idx, keep_a, got_a, keep_b, got_b):
    return call(
        factor_sum_y_kernel,
        "factor_sum_y",
        jax.ShapeDtypeStruct((8, TILE + PAD, BLOCK), bf16),
        [SMEM] + [VMEM] * 4,
        [pltpu.VMEM((8, TILE, BLOCK), f32)],
    )(idx, keep_a, got_a, keep_b, got_b)


def factor_sum_z_kernel(m, out):
    total = jnp.zeros(out.shape, f32)
    for z in range(8):
        total = total + decoded(m[z, 0:TILE, :]) * unscale_of(m[z, TILE:, 0:128])
    out[...] = total


def factor_sum_z(messages):
    return call(factor_sum_z_kernel, "factor_sum_z", shape(TILE, dtype=f32), [VMEM])(messages)


def proj_kernel(first, idx, a, b, basis, *rest):
    before, out = (None, rest[0]) if len(rest) == 1 else rest
    chan = idx[3] * 2 + idx[4]
    width = a.shape[1]
    flip, offset = first
    for c in range(3):
        cols = slice(c * 256, (c + 1) * 256)
        total = None if before is None else before[:, cols]
        for n, part in enumerate((a, b)):
            start = pl.multiple_of((chan ^ (flip + n)) * BLOCK + offset, 128)
            term = jnp.dot(part[...], basis[pl.ds(start, width), cols], preferred_element_type=f32)
            total = term if total is None else total + term
        out[:, cols] = total.astype(out.dtype)


def project(idx, first, a, b, basis, before, dtype):
    operands = (idx, a, b, basis) + (() if before is None else (before,))
    return call(
        functools.partial(proj_kernel, first),
        "project",
        shape(HW, dtype=dtype),
        [SMEM] + [VMEM] * (len(operands) - 1),
        flops=4 * HW * a.shape[1] * BLOCK,
        size=8 << 20,
    )(*operands)


def beside_kernel(act, basis, out):
    out[:, 0:QUARTER] = act[...]
    out[0:BLOCK, QUARTER:] = basis[...]
    out[BLOCK:, QUARTER:] = jnp.zeros((HW - BLOCK, QUARTER), bf16)


def side_by_side(act, basis):
    return call(beside_kernel, "beside", shape(HW, 2 * QUARTER), [VMEM] * 2)(act, basis)


def act_kernel(idx, b0, b1, b2, b3, pa, act, basis, part):
    chan = idx[3] * 2 + idx[4]
    blocks = (b0, b1, b2, b3)
    for m, block in enumerate(blocks):
        cols = slice(m * QUARTER, (m + 1) * QUARTER)
        basis[:, cols] = block[0:BLOCK, QUARTER:]
        part[cols, :] = crossed(block[:, 0:QUARTER], b0[:, 0:QUARTER]) * (1.0 / ROWS)
    for c in range(3):
        cols = slice(c * 256, (c + 1) * 256)
        total = None
        for m, block in enumerate(blocks):
            start = pl.multiple_of((chan ^ m) * QUARTER, 64)
            term = jnp.dot(
                block[:, 0:QUARTER],
                basis[pl.ds(start, QUARTER), cols],
                preferred_element_type=f32,
            )
            total = term if total is None else total + term
        pa[:, cols] = total.astype(bf16)
    for to in range(4):
        for y in range(2):
            for m in range(4):
                for h in range(2):
                    src = m * QUARTER + (h * 8 + y * 4 + to) * 12
                    dst = y * HALF + h * 12
                    act[to, dst : dst + 12, m * QUARTER : (m + 1) * QUARTER] = part[src : src + 12, :]


def act_parts(idx, blocks):
    return call(
        act_kernel,
        "act",
        [shape(HW), jax.ShapeDtypeStruct((4, 2 * HALF, BLOCK), f32)],
        [SMEM] + [VMEM] * 4,
        [pltpu.VMEM((BLOCK, BLOCK), bf16), pltpu.VMEM((BLOCK, QUARTER), f32)],
        flops=2 * HW * BLOCK * 960,
        size=4 << 20,
    )(idx, *blocks)


def scales_kernel(idx, pg, pa, act, o0, o1, o2, o3, p):
    x = idx[2]
    peak = jnp.zeros((1, 1), f32)
    for c in range(3):
        cols = slice(c * 256, (c + 1) * 256)
        tile = crossed(pg[...], pa[:, cols])
        tile = tile * tile * (1.0 / ROWS)
        p[:, cols] = tile
        peak = peak_of(tile, peak)
    e = exponent_of(peak)
    scale = scale_of(e)
    act_peak = jnp.zeros((1, 1), f32)
    for to in range(4):
        act_peak = peak_of(act[to], act_peak)
    act_e = exponent_of(act_peak)
    act_scale = scale_of(act_e)
    for d, out in enumerate((o0, o1, o2, o3)):
        to = lax.rem(x + d, 4)
        for hy in range(4):
            src = pl.multiple_of((hy * 4 + to) * TILE, TILE)
            out[hy * TILE : (hy + 1) * TILE, :] = coded(p[pl.ds(src, TILE), :] * scale).astype(bf16)
        out[4 * TILE : 5 * TILE, :] = coded(act[to] * act_scale).astype(bf16)
        out[5 * TILE :, :] = jnp.concatenate(
            [spread(e, 8, BLOCK), spread(act_e, 8, BLOCK)], axis=0
        ).astype(bf16)


def scales_messages(idx, pg, pa, act):
    return call(
        scales_kernel,
        "scales",
        [shape(5 * TILE + PAD)] * 4,
        [SMEM] + [VMEM] * 3,
        [pltpu.VMEM((BLOCK, BLOCK), f32)],
        flops=2 * HW * BLOCK * BLOCK,
        size=4 << 20,
    )(idx, pg, pa, act)


def scales_sum_x_kernel(idx, m0, m1, m2, m3, send, keep, keep_act, held, held_act):
    yl = idx[1]
    messages = (m0, m1, m2, m3)
    ends = [m[5 * TILE :, 0:128].astype(f32) for m in messages]
    factors = [unscale_of(end) for end in ends]
    act_factors = [unscale_of(end[8:, :]) for end in ends]

    def total(h, y):
        rows = pl.ds(pl.multiple_of((h * 2 + y) * TILE, TILE), TILE)
        parts = [decoded(m[rows, :]) * u for m, u in zip(messages, factors)]
        return (parts[0] + parts[1]) + (parts[2] + parts[3])

    peak = jnp.zeros((1, 1), f32)
    for h in range(2):
        keep[h * TILE : (h + 1) * TILE, :] = total(h, yl)
        out = total(h, 1 - yl)
        held[h * TILE : (h + 1) * TILE, :] = out
        peak = peak_of(out, peak)
    parts = [decoded(m[4 * TILE : 5 * TILE, :]) * u for m, u in zip(messages, act_factors)]
    held_act[...] = (parts[0] + parts[1]) + (parts[2] + parts[3])
    keep_act[...] = held_act[pl.ds(pl.multiple_of(yl * HALF, 8), HALF), :]
    out = held_act[pl.ds(pl.multiple_of((1 - yl) * HALF, 8), HALF), :]
    e = exponent_of(peak)
    act_e = exponent_of(peak_of(out, jnp.zeros((1, 1), f32)))
    send[0 : 2 * TILE, :] = coded(held[...] * scale_of(e)).astype(bf16)
    send[2 * TILE : 2 * TILE + 32, :] = jnp.concatenate(
        [coded(out * scale_of(act_e)), spread(e, 8, BLOCK)], axis=0
    ).astype(bf16)
    send[2 * TILE + 32 :, :] = spread(act_e, PAD, BLOCK).astype(bf16)


def scales_sum_x(idx, messages):
    return call(
        scales_sum_x_kernel,
        "scales_sum_x",
        [shape(2 * TILE + 32 + PAD), shape(2 * TILE, dtype=f32), shape(HALF, dtype=f32)],
        [SMEM] + [VMEM] * 4,
        [pltpu.VMEM((2 * TILE, BLOCK), f32), pltpu.VMEM((2 * HALF, BLOCK), f32)],
        size=2 << 20,
    )(idx, *messages)


def scales_sum_y_kernel(idx, keep, keep_act, got, out):
    chan = idx[3] * 2 + idx[4]
    end = got[2 * TILE : 2 * TILE + 32, :].astype(f32)
    act_end = got[2 * TILE + 32 :, 0:128].astype(f32)
    tile = keep[...] + decoded(got[0 : 2 * TILE, :]) * unscale_of(end[HALF:, :])
    act = keep_act[...] + decoded(end[0:HALF, :]) * unscale_of(act_end)
    e = exponent_of(peak_of(tile, jnp.zeros((1, 1), f32)))
    act_e = exponent_of(peak_of(act, jnp.zeros((1, 1), f32)))
    tile = coded(tile * scale_of(e)).astype(bf16)
    act = coded(act * scale_of(act_e))
    for h in range(2):
        for m in range(4):
            cols = slice(m * QUARTER, (m + 1) * QUARTER)
            out[h * 4 + (chan ^ m), 0:TILE, :] = tile[h * TILE : (h + 1) * TILE, cols]
            out[(chan ^ m) * 2 + h, TILE:, :] = jnp.concatenate(
                [act[h * 12 : (h + 1) * 12, cols], spread(e, 2, QUARTER), spread(act_e, 2, QUARTER)],
                axis=0,
            ).astype(bf16)


def scales_sum_y(idx, keep, keep_act, got):
    return call(
        scales_sum_y_kernel,
        "scales_sum_y",
        jax.ShapeDtypeStruct((8, TILE + 16, QUARTER), bf16),
        [SMEM] + [VMEM] * 3,
        size=1 << 20,
    )(idx, keep, keep_act, got)


def scales_sum_z_kernel(m, out, act):
    total = jnp.zeros((TILE, QUARTER), f32)
    total_act = jnp.zeros((12, QUARTER), f32)
    for z in range(8):
        end = m[z, TILE:, :].astype(f32)
        total = total + decoded(m[z, 0:TILE, :]) * unscale_of(end[12:14, :])
        total_act = total_act + decoded(end[0:12, :]) * unscale_of(end[14:16, :])
    out[...] = total
    act[...] = total_act


def scales_sum_z(messages):
    return call(
        scales_sum_z_kernel,
        "scales_sum_z",
        [shape(TILE, QUARTER, f32), shape(12, QUARTER, f32)],
        [VMEM],
        size=1 << 18,
    )(messages)


def after(value, *earlier):
    return lax.optimization_barrier((value,) + earlier)[0]


def swap(value, axis):
    return lax.ppermute(value, axis, [(0, 1), (1, 0)])


def along_x(messages):
    return [messages[0]] + [
        lax.ppermute(messages[d], "x", [(i, (i + d) % 4) for i in range(4)]) for d in (1, 3, 2)
    ]


def scales_places():
    return [
        (z * 4 + k, (2 * k + z // 4) * 4 + z % 4) for z in range(8) for k in range(4)
    ]


def on_device(activations, gradients, basis_act, basis_grad):
    z, yl, x, yh, core = [lax.axis_index(a) for a in AXES]
    idx = jnp.stack([z, yl, x, yh, core]).astype(jnp.int32)

    grad_far = swap(gradients, "yh")
    grad_other = swap(gradients, "core")
    both = side_by_side(activations, basis_act)
    both_other = swap(both, "core")

    msg_a = factor_messages(idx, gradients, gradients, grad_other)
    got_a = along_x(msg_a)
    proj = project(idx, (0, 0), after(gradients, both_other, *msg_a), grad_other, basis_grad, None, f32)

    grad_far, proj = lax.optimization_barrier((grad_far, proj))
    grad_far_other = swap(after(grad_far, *got_a[1:3]), "core")
    both_far = swap(after(both, grad_far), "yh")
    msg_b = factor_messages(idx, gradients, grad_far, grad_far_other)
    proj, *got_a = lax.optimization_barrier((proj,) + tuple(got_a) + tuple(msg_b))[:5]
    got_b = along_x(msg_b)
    proj_grad = project(idx, (2, 0), grad_far, grad_far_other, basis_grad, proj, bf16)
    both_far_other = swap(after(both_far, proj_grad), "core")

    proj_act, act = act_parts(idx, (both, both_other, both_far, both_far_other))
    msg_e = scales_messages(idx, proj_grad, proj_act, act)
    got_e = along_x(msg_e)

    send_a, keep_a = factor_sum_x(idx, [after(got_a[0], *msg_e)] + list(got_a[1:]))
    y_a = swap(send_a, "yl")
    send_b, keep_b = factor_sum_x(idx, [after(got_b[0], send_a)] + got_b[1:])
    y_b = swap(send_b, "yl")
    to_z = factor_sum_y(idx, keep_a, y_a, keep_b, y_b)
    z_cov = lax.all_to_all(to_z, "z", 0, 0)
    grad_factor = factor_sum_z(z_cov)

    send_e, keep_e, keep_act = scales_sum_x(idx, [after(got_e[0], to_z)] + got_e[1:])
    y_e = swap(send_e, "yl")
    z_e = lax.all_to_all(after(scales_sum_y(idx, keep_e, keep_act, y_e), z_cov), "z", 0, 0)
    scales, act_factor = scales_sum_z(z_e)
    eigen_scales = lax.ppermute(scales, ("z", "yh", "core"), scales_places())
    return act_factor, grad_factor, eigen_scales


def solution(mesh):
    fine = Mesh(mesh.devices.reshape(SIZES), AXES)
    return jax.shard_map(
        on_device,
        mesh=fine,
        in_specs=(P(SAMP, CHAN), P(SAMP, CHAN), P(None, CHAN), P(None, CHAN)),
        out_specs=(P(SAMP, CHAN), P(SAMP, CHAN), P(SAMP, CHAN)),
        check_vma=False,
    )
```

time: 1370 us -> 157 us (0.11)
  waiting for transfers between devices: 1310 us -> 63.1 us
  Pallas kernels: 0 us -> 41.2 us
  matrix products: 29.7 us -> 0 us
  starting transfers between devices: 0.24 us -> 29.1 us
  blocking collectives: 0 us -> 17.2 us
    reduce_scatter x2 -> x0, waiting for transfers between devices: 643 us -> none  [the longest x1 333 us: on_device(): lax.psum_scatter(partial_grad, 'samp', scatter_dimension=1, tiled=True)]
    psum x1 -> x0, waiting for transfers between devices: 562 us -> none  [on_device(): summed = lax.psum(crossed(full_act, activations) * inverse, 'samp')]
    all_gather x3 -> x0, waiting for transfers between devices: 107 us -> none  [the longest x1 46.9 us: on_device(): full_grad = lax.all_gather(gradients, 'chan', axis=1, tiled=True)]
    ppermute x0 -> x19, waiting for transfers between devices: none -> 63.1 us  [the longest x9 29.8 us: along_x(): lax.ppermute(messages[d], 'x', [(i, (i + d) % 4) for i in range(4)])]
    pallas_call x0 -> x14, Pallas kernels: none -> 41.2 us  [the longest x2 10.9 us: factor_messages(): call(factor_kernel, 'factor', [shape(8 * TILE + PAD)] * 4, [SMEM] + [VMEM...]
    dot_general x4 -> x0, matrix products: 29.7 us -> none  [the longest x2 14.2 us: crossed(): lax.dot_general(left, right, (((0,), (0,)), ((), ())), preferred_element_...]
    ppermute x0 -> x19, starting transfers between devices: none -> 20.6 us  [the longest x9 12 us: along_x(): lax.ppermute(messages[d], 'x', [(i, (i + d) % 4) for i in range(4)])]
    all_to_all x0 -> x1, blocking collectives: none -> 17.2 us  [on_device(): lax.all_to_all(after(scales_sum_y(idx, keep_e, keep_act, y_e), z_cov), 'z...]
  transfers between devices with their start and end apart: 6 -> 20, of which waited for: 6 -> 12; matrix products, arithmetic and copies ran while one was open for 2% -> 0% of each run, Pallas kernels for 0% -> 24%
where the time goes in v1:
time: 157 us
  waiting for transfers between devices  63.1 us (40%)
  Pallas kernels  41.2 us (26%)
  starting transfers between devices  29.1 us (19%)
  blocking collectives  17.2 us (11%)
  local copies, waits for them, and re-layouts  5.31 us (3%)
    ppermute x9, waiting for transfers between devices, along_x(): lax.ppermute(messages[d], 'x', [(i, (i + d) % 4) for i in range(4)])  29.8 us
    ppermute x9, waiting for transfers between devices, swap(): return lax.ppermute(value, axis, [(0, 1), (1, 0)])  27.9 us
    all_to_all x1, blocking collectives, on_device(): lax.all_to_all(after(scales_sum_y(idx, keep_e, keep_act, y_e), z_cov), 'z...  17.2 us
    ppermute x9, starting transfers between devices, along_x(): lax.ppermute(messages[d], 'x', [(i, (i + d) % 4) for i in range(4)])  12 us
    pallas_call x2, Pallas kernels, factor_messages(): call(factor_kernel, 'factor', [shape(8 * TILE + PAD)] * 4, [SMEM] + [VMEM...  10.9 us
    pallas_call x2, Pallas kernels, project(): call(functools.partial(proj_kernel, first), 'project', shape(HW, dtype=dt...  8.84 us
    all_to_all x1, starting transfers between devices, on_device(): z_cov = lax.all_to_all(to_z, 'z', 0, 0)  8.47 us
    pallas_call x2, Pallas kernels, factor_sum_x(): call(factor_sum_x_kernel, 'factor_sum_x', [shape(4 * TILE + PAD), shape(4...  7.48 us
  transfers between devices with their start and end apart: 20, of which 12 were waited for; matrix products, arithmetic and copies ran while one was open for 0% of the time, Pallas kernels for 24%

profile of v1, /device:TPU:26, one launch (start us, length us, event | category | flops | bytes accessed | tf_op | source)
XLA Modules:
  0.0 156.7 jit_solution(1251702014788593336)
XLA Ops:
  0.7 1.3 collective-permute-start
  2.1 1.7 %collective-permute-done.2.other.b = bf16[784,768]{1,0:T(8,128)(2,1)S(1)} collective-permute-done((bf16[784,768]{1,0:T(8,128)(2,1)}, bf16[784,768]{1,0:T(8,128)(2,1)S(1)}, u32[]{:S(2)}, u32[]{:S(2)}) %collective-permute-start.2) | collective-permute-done | bytes 1204256 | tf_op jit(solution)/shard_map/ppermute | solution.py:397
  3.8 1.3 copy-done
  5.1 5.4 %factor.2 = (bf16[400,768]{1,0:T(8,128)(2,1)S(1)}, bf16[400,768]{1,0:T(8,128)(2,1)}, bf16[400,768]{1,0:T(8,128)(2,1)S(1)}, bf16[400,768]{1,0:T(8,128)(2,1)}) custom-call(s32[5]{0:T(128)S(1)} %stack.23.idx, bf16[784,768]{1,0:T(8,128)(2,1)S(1)} %copy-done, bf16[784,768]{1,0:T(8,128)(2,1)S(1)} %copy-done, bf16[784,768]{1,0:T(8,128)(2,1)S(1)} %collective-permute-done.2.other.b), custom_call_target="tpu_custom_call" | custom-call | flops 1 | bytes 1 | tf_op jit(solution)/shard_map/factor/pallas_call | solution.py:106
  10.6 0.8 copy-done.4
  11.4 0.8 copy-done.6
  12.2 1.5 collective-permute-start.3
  13.7 0.5 collective-permute-start.4
  14.9 2.0 %collective-permute-done.1.b1 = bf16[784,384]{1,0:T(8,128)(2,1)S(1)} collective-permute-done((bf16[784,384]{1,0:T(8,128)(2,1)S(1)}, bf16[784,384]{1,0:T(8,128)(2,1)S(1)}, u32[]{:S(2)}, u32[]{:S(2)}) %collective-permute-start.1) | collective-permute-done | bytes 602144 | tf_op jit(solution)/shard_map/ppermute | solution.py:397
  16.9 1.3 copy-done.3
  18.2 4.4 %project.2.rest_0_ = f32[784,768]{1,0:T(8,128)S(1)} custom-call(s32[5]{0:T(128)S(1)} %stack.23.idx, bf16[784,768]{1,0:T(8,128)(2,1)S(1)} %copy-done.1, bf16[784,768]{1,0:T(8,128)(2,1)S(1)} %copy-done.3, bf16[3072,768]{1,0:T(8,128)(2,1)} %basis.4), custom_call_target="tpu_custom_call" | custom-call | flops 1 | bytes 1 | tf_op jit(solution)/shard_map/project/pallas_call | solution.py:200
  22.7 8.7 %collective-permute-done.same.a = bf16[784,768]{1,0:T(8,128)(2,1)S(1)} collective-permute-done((bf16[784,768]{1,0:T(8,128)(2,1)}, bf16[784,768]{1,0:T(8,128)(2,1)S(1)}, u32[]{:S(2)}, u32[]{:S(2)}) %collective-permute-start) | collective-permute-done | bytes 1204256 | tf_op jit(solution)/shard_map/ppermute | solution.py:397
  31.4 2.2 %collective-permute-start.6 = (bf16[400,768]{1,0:T(8,128)(2,1)S(1)}, bf16[400,768]{1,0:T(8,128)(2,1)S(1)}, u32[]{:S(2)}, u32[]{:S(2)}) collective-permute-start(bf16[400,768]{1,0:T(8,128)(2,1)S(1)} %copy-done.7), channel_id=1, source_target_pairs={{0,8},{4,12},{8,0},{12,4},{1,9},{5,13},{9,1},{13,5},{2,10},{6,14},... | collective-permute-start | bytes 1843208 | tf_op jit(solution)/shard_map/ppermute | solution.py:402
  33.6 1.2 collective-permute-start.7
  34.8 5.5 %factor.3 = (bf16[400,768]{1,0:T(8,128)(2,1)S(1)}, bf16[400,768]{1,0:T(8,128)(2,1)}, bf16[400,768]{1,0:T(8,128)(2,1)S(1)}, bf16[400,768]{1,0:T(8,128)(2,1)}) custom-call(s32[5]{0:T(128)S(1)} %stack.23.idx, bf16[784,768]{1,0:T(8,128)(2,1)S(1)} %copy-done.1, bf16[784,768]{1,0:T(8,128)(2,1)S(1)} %collective-permute-done.same.a, ...), custom_call_target="tpu_custom_call" | custom-call | flops 1 | bytes 1 | tf_op jit(solution)/shard_map/factor/pallas_call | solution.py:106
  40.3 0.9 collective-permute-start.10
  41.2 1.1 collective-permute-start.11
  42.3 1.5 collective-permute-start.12
  43.9 5.8 %collective-permute-done.6.m3 = bf16[400,768]{1,0:T(8,128)(2,1)S(1)} collective-permute-done((bf16[400,768]{1,0:T(8,128)(2,1)S(1)}, bf16[400,768]{1,0:T(8,128)(2,1)S(1)}, u32[]{:S(2)}, u32[]{:S(2)}) %collective-permute-start.6) | collective-permute-done | bytes 614432 | tf_op jit(solution)/shard_map/ppermute | solution.py:402
  49.7 4.4 %project.3.pg = bf16[784,768]{1,0:T(8,128)(2,1)S(1)} custom-call(s32[5]{0:T(128)S(1)} %stack.23.idx, bf16[784,768]{1,0:T(8,128)(2,1)S(1)} %collective-permute-done.same.a, bf16[784,768]{1,0:T(8,128)(2,1)S(1)} %collective-permute-done.5.other.b, bf16[3072,768]{1,0:T(8,128)(2,1)} %basis.4, f32[784,768]{1,0:T(8,128)S(1)} %project.2.rest_0_), custom_call_target="tpu_custom_call" | custom-call | flops 1 | bytes 1 | tf_op jit(solution)/shard_map/project/pallas_call | solution.py:200
  54.1 0.3 collective-permute-start.8
  54.4 2.0 %collective-permute-done.8.b3 = bf16[784,384]{1,0:T(8,128)(2,1)S(1)} collective-permute-done((bf16[784,384]{1,0:T(8,128)(2,1)S(1)}, bf16[784,384]{1,0:T(8,128)(2,1)S(1)}, u32[]{:S(2)}, u32[]{:S(2)}) %collective-permute-start.8) | collective-permute-done | bytes 602144 | tf_op jit(solution)/shard_map/ppermute | solution.py:397
  56.4 2.8 %act.2 = (bf16[784,768]{1,0:T(8,128)(2,1)S(1)}, f32[4,48,768]{2,1,0:T(8,128)S(1)}) custom-call(s32[5]{0:T(128)S(1)} %stack.23.idx, bf16[784,384]{1,0:T(8,128)(2,1)S(1)} %beside.1.b0, bf16[784,384]{1,0:T(8,128)(2,1)S(1)} %collective-permute-done.1.b1, bf16[784,384]{1,0:T(8,128)(2,1)S(1)} %collective-permute-done.7.b2, ...), custom_call_target="tpu_custom_call" | custom-call | flops 1 | bytes 1 | tf_op jit(solution)/shard_map/act/pallas_call | solution.py:249
  59.3 2.9 %scales.1 = (bf16[256,768]{1,0:T(8,128)(2,1)S(1)}, bf16[256,768]{1,0:T(8,128)(2,1)S(1)}, bf16[256,768]{1,0:T(8,128)(2,1)S(1)}, bf16[256,768]{1,0:T(8,128)(2,1)S(1)}) custom-call(s32[5]{0:T(128)S(1)} %stack.23.idx, bf16[784,768]{1,0:T(8,128)(2,1)S(1)} %project.3.pg, bf16[784,768]{1,0:T(8,128)(2,1)S(1)} %get-tuple-element.56.pa, ...), custom_call_target="tpu_custom_call" | custom-call | flops 1 | bytes 1 | tf_op jit(solution)/shard_map/scales/pallas_call | solution.py:288
  62.2 4.1 %factor_sum_x.2 = (bf16[208,768]{1,0:T(8,128)(2,1)S(1)}, f32[192,768]{1,0:T(8,128)S(1)}) custom-call(s32[5]{0:T(128)S(1)} %stack.23.idx, bf16[400,768]{1,0:T(8,128)(2,1)S(1)} %copy-done.5, bf16[400,768]{1,0:T(8,128)(2,1)} %collective-permute-done.3.m1, bf16[400,768]{1,0:T(8,128)(2,1)} %collective-permute-done.4.m2, ...), custom_call_target="tpu_custom_call" | custom-call | flops 1 | bytes 1 | tf_op jit(solution)/shard_map/factor_sum_x/pallas_call | solution.py:136
  66.3 0.8 collective-permute-start.9
  67.2 8.4 %collective-permute-done.12.m3 = bf16[400,768]{1,0:T(8,128)(2,1)S(1)} collective-permute-done((bf16[400,768]{1,0:T(8,128)(2,1)S(1)}, bf16[400,768]{1,0:T(8,128)(2,1)S(1)}, u32[]{:S(2)}, u32[]{:S(2)}) %collective-permute-start.12) | collective-permute-done | bytes 614432 | tf_op jit(solution)/shard_map/ppermute | solution.py:402
  75.5 3.4 %factor_sum_x.3 = (bf16[208,768]{1,0:T(8,128)(2,1)S(1)}, f32[192,768]{1,0:T(8,128)S(1)}) custom-call(s32[5]{0:T(128)S(1)} %stack.23.idx, bf16[400,768]{1,0:T(8,128)(2,1)S(1)} %get-tuple-element.69.m0, bf16[400,768]{1,0:T(8,128)(2,1)S(1)} %collective-permute-done.10.m1, bf16[400,768]{1,0:T(8,128)(2,1)S(1)} %collective-permute-done.11.m2, ...), custom_call_target="tpu_custom_call" | custom-call | flops 1 | bytes 1 | tf_op jit(solution)/shard_map/factor_sum_x/pallas_call | solution.py:136
  78.9 0.8 collective-permute-start.13
  79.8 8.3 %collective-permute-done.13.got_b = bf16[208,768]{1,0:T(8,128)(2,1)S(1)} collective-permute-done((bf16[208,768]{1,0:T(8,128)(2,1)S(1)}, bf16[208,768]{1,0:T(8,128)(2,1)S(1)}, u32[]{:S(2)}, u32[]{:S(2)}) %collective-permute-start.13) | collective-permute-done | bytes 319520 | tf_op jit(solution)/shard_map/ppermute | solution.py:397
  88.1 2.5 %factor_sum_y.1 = bf16[8,64,768]{2,1,0:T(8,128)(2,1)} custom-call(s32[5]{0:T(128)S(1)} %stack.23.idx, f32[192,768]{1,0:T(8,128)S(1)} %get-tuple-element.67.keep_a, bf16[208,768]{1,0:T(8,128)(2,1)S(1)} %collective-permute-done.9.got_a, f32[192,768]{1,0:T(8,128)S(1)} %get-tuple-element.70.keep_b, bf16[208,768]{1,0:T(8,128)(2,1)S(1)} %collective-permute-done.13.got_b), custom_call_target="tpu_custom_call" | custom-call | flops 1 | bytes 1 | tf_op jit(solution)/shard_map/factor_sum_y/pallas_call | solution.py:163
  90.6 8.5 %all-to-all-start = ((bf16[8,64,768]{2,1,0:T(8,128)(2,1)}), bf16[8,64,768]{2,1,0:T(8,128)(2,1)S(1)}, u32[]{:S(2)}, u32[]{:S(2)}) async-start(bf16[8,64,768]{2,1,0:T(8,128)(2,1)} %factor_sum_y.1), calls=%async_computation | async-start | bytes 1572864 | tf_op jit(solution)/shard_map/all_to_all | solution.py:443
  99.1 1.5 collective-permute-start.14
  100.6 0.5 collective-permute-start.15
  101.1 2.1 %collective-permute-start.16 = (bf16[256,768]{1,0:T(8,128)(2,1)S(1)}, bf16[256,768]{1,0:T(8,128)(2,1)S(1)}, u32[]{:S(2)}, u32[]{:S(2)}) collective-permute-start(bf16[256,768]{1,0:T(8,128)(2,1)S(1)} %get-tuple-element.61), channel_id=1, source_target_pairs={{0,8},{4,12},{8,0},{12,4},{1,9},{5,13},{9,1},{13,5},{2,10},{6,14},... | collective-permute-start | bytes 1179656 | tf_op jit(solution)/shard_map/ppermute | solution.py:402
  103.2 7.9 %collective-permute-done.14.m1 = bf16[256,768]{1,0:T(8,128)(2,1)S(1)} collective-permute-done((bf16[256,768]{1,0:T(8,128)(2,1)S(1)}, bf16[256,768]{1,0:T(8,128)(2,1)S(1)}, u32[]{:S(2)}, u32[]{:S(2)}) %collective-permute-start.14) | collective-permute-done | bytes 393248 | tf_op jit(solution)/shard_map/ppermute | solution.py:402
  111.1 0.9 collective-permute-done.15.m2
  112.0 6.8 %collective-permute-done.16.m3 = bf16[256,768]{1,0:T(8,128)(2,1)S(1)} collective-permute-done((bf16[256,768]{1,0:T(8,128)(2,1)S(1)}, bf16[256,768]{1,0:T(8,128)(2,1)S(1)}, u32[]{:S(2)}, u32[]{:S(2)}) %collective-permute-start.16) | collective-permute-done | bytes 393248 | tf_op jit(solution)/shard_map/ppermute | solution.py:402
  118.8 2.3 %scales_sum_x.1 = (bf16[144,768]{1,0:T(8,128)(2,1)S(1)}, f32[96,768]{1,0:T(8,128)S(1)}, f32[24,768]{1,0:T(8,128)S(1)}) custom-call(s32[5]{0:T(128)S(1)} %stack.23.idx, bf16[256,768]{1,0:T(8,128)(2,1)S(1)} %get-tuple-element.72.m0, bf16[256,768]{1,0:T(8,128)(2,1)S(1)} %collective-permute-done.14.m1, bf16[256,768]{1,0:T(8,128)(2,1)S(1)} %collective-permute-done.15.m2, ...), custom_call_target="tpu_custom_call" | custom-call | flops 1 | bytes 1 | tf_op jit(solution)/shard_map/scales_sum_x/pallas_call | solution.py:331
  121.1 0.8 collective-permute-start.17
  122.0 5.2 %collective-permute-done.17.got = bf16[144,768]{1,0:T(8,128)(2,1)S(1)} collective-permute-done((bf16[144,768]{1,0:T(8,128)(2,1)S(1)}, bf16[144,768]{1,0:T(8,128)(2,1)S(1)}, u32[]{:S(2)}, u32[]{:S(2)}) %collective-permute-start.17) | collective-permute-done | bytes 221216 | tf_op jit(solution)/shard_map/ppermute | solution.py:397
  127.1 1.0 scales_sum_y.1
  128.2 17.2 %all_to_all.10.m = bf16[8,64,192]{2,1,0:T(8,128)(2,1)S(1)} all-to-all(bf16[8,64,192]{2,1,0:T(8,128)(2,1)S(1)} %scales_sum_y.1), channel_id=1, replica_groups=mesh['z'=8,'yl'=2,'x'=4,'yh'=2,'core'=2] {'z'}, dimensions={0} | all-to-all | bytes 393216 | tf_op jit(solution)/shard_map/all_to_all | solution.py:448
  145.4 0.9 scales_sum_z.1
  146.3 3.1 %collective-permute-start.18 = (f32[48,192]{1,0:T(8,128)S(1)}, f32[48,192]{1,0:T(8,128)S(1)}, u32[]{:S(2)}, u32[]{:S(2)}) collective-permute-start(f32[48,192]{1,0:T(8,128)S(1)} %get-tuple-element.78), channel_id=1, source_target_pairs={{0,0},{1,64},{2,128},{3,192},{32,1},{33,65},{34,129},{35,193},{64,... | collective-permute-start | bytes 110600 | tf_op jit(solution)/shard_map/ppermute | solution.py:450
  149.4 1.3 factor_sum_z.1
  150.7 5.4 %collective-permute-done.18 = f32[48,192]{1,0:T(8,128)S(1)} collective-permute-done((f32[48,192]{1,0:T(8,128)S(1)}, f32[48,192]{1,0:T(8,128)S(1)}, u32[]{:S(2)}, u32[]{:S(2)}) %collective-permute-start.18) | collective-permute-done | bytes 36896 | tf_op jit(solution)/shard_map/ppermute | solution.py:450
  156.1 0.6 copy.10
  (31 shorter events, 0.9 us)
Async XLA Ops:
  0.6 3.2 %collective-permute-start.2 = (bf16[784,768]{1,0:T(8,128)(2,1)}, bf16[784,768]{1,0:T(8,128)(2,1)S(1)}, u32[]{:S(2)}, u32[]{:S(2)}) collective-permute-start(bf16[784,768]{1,0:T(8,128)(2,1)} %own.3), channel_id=1, source_target_pairs={{0,1},{1,0},{2,3},{3,2},{4,5},{5,4},{6,7},{7,6},{8,9},{9,8},{10,11... | collective-permute-start | bytes 3612680 | tf_op jit(solution)/shard_map/ppermute | solution.py:397
  0.7 30.6 %collective-permute-start = (bf16[784,768]{1,0:T(8,128)(2,1)}, bf16[784,768]{1,0:T(8,128)(2,1)S(1)}, u32[]{:S(2)}, u32[]{:S(2)}) collective-permute-start(bf16[784,768]{1,0:T(8,128)(2,1)} %own.3), channel_id=1, source_target_pairs={{0,2},{2,0},{1,3},{3,1},{4,6},{6,4},{5,7},{7,5},{8,10},{10,8},{9,1... | collective-permute-start | bytes 3612680 | tf_op jit(solution)/shard_map/ppermute | solution.py:397
  3.8 1.3 copy-start
  5.1 5.5 %copy-start.2 = (bf16[784,768]{1,0:T(8,128)(2,1)}, bf16[784,768]{1,0:T(8,128)(2,1)S(1)}, u32[]{:S(2)}) copy-start(bf16[784,768]{1,0:T(8,128)(2,1)S(1)} %collective-permute-done.2.other.b) | copy-start | bytes 3612676
  5.1 9.2 %copy-start.8 = (bf16[784,192]{0,1:T(8,128)(2,1)S(1)}, bf16[784,192]{0,1:T(8,128)(2,1)}, u32[]{:S(2)}) copy-start(bf16[784,192]{0,1:T(8,128)(2,1)} %param.4) | copy-start | bytes 903172
  5.1 9.3 %copy-start.9 = (bf16[768,192]{0,1:T(8,128)(2,1)S(1)}, bf16[768,192]{0,1:T(8,128)(2,1)}, u32[]{:S(2)}) copy-start(bf16[768,192]{0,1:T(8,128)(2,1)} %param.6) | copy-start | bytes 884740
  10.5 0.8 copy-start.4
  11.4 0.8 copy-start.6
  12.2 19.1 %collective-permute-start.3 = (bf16[400,768]{1,0:T(8,128)(2,1)}, bf16[400,768]{1,0:T(8,128)(2,1)}, u32[]{:S(2)}, u32[]{:S(2)}) collective-permute-start(bf16[400,768]{1,0:T(8,128)(2,1)} %get-tuple-element.42), channel_id=1, source_target_pairs={{0,4},{4,8},{8,12},{12,0},{1,5},{5,9},{9,13},{13,1},{2,6},{6,10},{... | collective-permute-start | bytes 1843208 | tf_op jit(solution)/shard_map/ppermute | solution.py:402
  13.7 17.7 %collective-permute-start.4 = (bf16[400,768]{1,0:T(8,128)(2,1)}, bf16[400,768]{1,0:T(8,128)(2,1)}, u32[]{:S(2)}, u32[]{:S(2)}) collective-permute-start(bf16[400,768]{1,0:T(8,128)(2,1)} %get-tuple-element.44), channel_id=1, source_target_pairs={{0,12},{4,0},{8,4},{12,8},{1,13},{5,1},{9,5},{13,9},{2,14},{6,2},{... | collective-permute-start | bytes 1843208 | tf_op jit(solution)/shard_map/ppermute | solution.py:402
  14.4 2.5 %copy-start.1 = (bf16[784,768]{1,0:T(8,128)(2,1)S(1)}, bf16[784,768]{1,0:T(8,128)(2,1)}, u32[]{:S(2)}) copy-start(bf16[784,768]{1,0:T(8,128)(2,1)} %own.3) | copy-start | bytes 3612676
  14.8 2.1 %collective-permute-start.1 = (bf16[784,384]{1,0:T(8,128)(2,1)S(1)}, bf16[784,384]{1,0:T(8,128)(2,1)S(1)}, u32[]{:S(2)}, u32[]{:S(2)}) collective-permute-start(bf16[784,384]{1,0:T(8,128)(2,1)S(1)} %beside.1.b0), channel_id=1, source_target_pairs={{0,1},{1,0},{2,3},{3,2},{4,5},{5,4},{6,7},{7,6},{8,9},{9,8},{10,11... | collective-permute-start | bytes 1806344 | tf_op jit(solution)/shard_map/ppermute | solution.py:397
  16.9 1.3 copy-start.3
  18.2 13.2 %copy-start.7 = (bf16[400,768]{1,0:T(8,128)(2,1)S(1)}, bf16[400,768]{1,0:T(8,128)(2,1)}, u32[]{:S(2)}) copy-start(bf16[400,768]{1,0:T(8,128)(2,1)} %copy-done.6) | copy-start | bytes 1843204
  31.4 3.5 %collective-permute-start.5 = (bf16[784,768]{1,0:T(8,128)(2,1)S(1)}, bf16[784,768]{1,0:T(8,128)(2,1)S(1)}, u32[]{:S(2)}, u32[]{:S(2)}) collective-permute-start(bf16[784,768]{1,0:T(8,128)(2,1)S(1)} %collective-permute-done.same.a), channel_id=1, source_target_pairs={{0,1},{1,0},{2,3},{3,2},{4,5},{5,4},{6,7},{7,6},{8,9},{9,8},{10,11... | collective-permute-start | bytes 3612680 | tf_op jit(solution)/shard_map/ppermute | solution.py:397
  31.4 18.3 %collective-permute-start.6 = (bf16[400,768]{1,0:T(8,128)(2,1)S(1)}, bf16[400,768]{1,0:T(8,128)(2,1)S(1)}, u32[]{:S(2)}, u32[]{:S(2)}) collective-permute-start(bf16[400,768]{1,0:T(8,128)(2,1)S(1)} %copy-done.7), channel_id=1, source_target_pairs={{0,8},{4,12},{8,0},{12,4},{1,9},{5,13},{9,1},{13,5},{2,10},{6,14},... | collective-permute-start | bytes 1843208 | tf_op jit(solution)/shard_map/ppermute | solution.py:402
  33.6 20.5 %collective-permute-start.7 = (bf16[784,384]{1,0:T(8,128)(2,1)S(1)}, bf16[784,384]{1,0:T(8,128)(2,1)S(1)}, u32[]{:S(2)}, u32[]{:S(2)}) collective-permute-start(bf16[784,384]{1,0:T(8,128)(2,1)S(1)} %beside.1.b0), channel_id=1, source_target_pairs={{0,2},{2,0},{1,3},{3,1},{4,6},{6,4},{5,7},{7,5},{8,10},{10,8},{9,1... | collective-permute-start | bytes 1806344 | tf_op jit(solution)/shard_map/ppermute | solution.py:397
  40.3 26.9 %collective-permute-start.10 = (bf16[400,768]{1,0:T(8,128)(2,1)}, bf16[400,768]{1,0:T(8,128)(2,1)S(1)}, u32[]{:S(2)}, u32[]{:S(2)}) collective-permute-start(bf16[400,768]{1,0:T(8,128)(2,1)} %get-tuple-element.50), channel_id=1, source_target_pairs={{0,4},{4,8},{8,12},{12,0},{1,5},{5,9},{9,13},{13,1},{2,6},{6,10},{... | collective-permute-start | bytes 1843208 | tf_op jit(solution)/shard_map/ppermute | solution.py:402
  41.2 26.0 %collective-permute-start.11 = (bf16[400,768]{1,0:T(8,128)(2,1)}, bf16[400,768]{1,0:T(8,128)(2,1)S(1)}, u32[]{:S(2)}, u32[]{:S(2)}) collective-permute-start(bf16[400,768]{1,0:T(8,128)(2,1)} %get-tuple-element.52), channel_id=1, source_target_pairs={{0,12},{4,0},{8,4},{12,8},{1,13},{5,1},{9,5},{13,9},{2,14},{6,2},{... | collective-permute-start | bytes 1843208 | tf_op jit(solution)/shard_map/ppermute | solution.py:402
  42.3 33.2 %collective-permute-start.12 = (bf16[400,768]{1,0:T(8,128)(2,1)S(1)}, bf16[400,768]{1,0:T(8,128)(2,1)S(1)}, u32[]{:S(2)}, u32[]{:S(2)}) collective-permute-start(bf16[400,768]{1,0:T(8,128)(2,1)S(1)} %get-tuple-element.51), channel_id=1, source_target_pairs={{0,8},{4,12},{8,0},{12,4},{1,9},{5,13},{9,1},{13,5},{2,10},{6,14},... | collective-permute-start | bytes 1843208 | tf_op jit(solution)/shard_map/ppermute | solution.py:402
  54.1 2.3 %collective-permute-start.8 = (bf16[784,384]{1,0:T(8,128)(2,1)S(1)}, bf16[784,384]{1,0:T(8,128)(2,1)S(1)}, u32[]{:S(2)}, u32[]{:S(2)}) collective-permute-start(bf16[784,384]{1,0:T(8,128)(2,1)S(1)} %collective-permute-done.7.b2), channel_id=1, source_target_pairs={{0,1},{1,0},{2,3},{3,2},{4,5},{5,4},{6,7},{7,6},{8,9},{9,8},{10,11... | collective-permute-start | bytes 1806344 | tf_op jit(solution)/shard_map/ppermute | solution.py:397
  59.3 2.9 %copy-start.5 = (bf16[400,768]{1,0:T(8,128)(2,1)S(1)}, bf16[400,768]{1,0:T(8,128)(2,1)}, u32[]{:S(2)}) copy-start(bf16[400,768]{1,0:T(8,128)(2,1)} %copy-done.4) | copy-start | bytes 1843204
  66.3 13.4 %collective-permute-start.9 = (bf16[208,768]{1,0:T(8,128)(2,1)S(1)}, bf16[208,768]{1,0:T(8,128)(2,1)S(1)}, u32[]{:S(2)}, u32[]{:S(2)}) collective-permute-start(bf16[208,768]{1,0:T(8,128)(2,1)S(1)} %get-tuple-element.68), channel_id=1, source_target_pairs={{0,16},{16,0},{1,17},{17,1},{2,18},{18,2},{3,19},{19,3},{4,20},{20... | collective-permute-start | bytes 958472 | tf_op jit(solution)/shard_map/ppermute | solution.py:397
  78.9 9.2 %collective-permute-start.13 = (bf16[208,768]{1,0:T(8,128)(2,1)S(1)}, bf16[208,768]{1,0:T(8,128)(2,1)S(1)}, u32[]{:S(2)}, u32[]{:S(2)}) collective-permute-start(bf16[208,768]{1,0:T(8,128)(2,1)S(1)} %get-tuple-element.71), channel_id=1, source_target_pairs={{0,16},{16,0},{1,17},{17,1},{2,18},{18,2},{3,19},{19,3},{4,20},{20... | collective-permute-start | bytes 958472 | tf_op jit(solution)/shard_map/ppermute | solution.py:397
  90.6 37.6 %all-to-all-start = ((bf16[8,64,768]{2,1,0:T(8,128)(2,1)}), bf16[8,64,768]{2,1,0:T(8,128)(2,1)S(1)}, u32[]{:S(2)}, u32[]{:S(2)}) async-start(bf16[8,64,768]{2,1,0:T(8,128)(2,1)} %factor_sum_y.1), calls=%async_computation | async-start | bytes 1572864 | tf_op jit(solution)/shard_map/all_to_all | solution.py:443
  99.1 12.1 %collective-permute-start.14 = (bf16[256,768]{1,0:T(8,128)(2,1)S(1)}, bf16[256,768]{1,0:T(8,128)(2,1)S(1)}, u32[]{:S(2)}, u32[]{:S(2)}) collective-permute-start(bf16[256,768]{1,0:T(8,128)(2,1)S(1)} %get-tuple-element.60), channel_id=1, source_target_pairs={{0,4},{4,8},{8,12},{12,0},{1,5},{5,9},{9,13},{13,1},{2,6},{6,10},{... | collective-permute-start | bytes 1179656 | tf_op jit(solution)/shard_map/ppermute | solution.py:402
  100.6 11.4 %collective-permute-start.15 = (bf16[256,768]{1,0:T(8,128)(2,1)S(1)}, bf16[256,768]{1,0:T(8,128)(2,1)S(1)}, u32[]{:S(2)}, u32[]{:S(2)}) collective-permute-start(bf16[256,768]{1,0:T(8,128)(2,1)S(1)} %get-tuple-element.62), channel_id=1, source_target_pairs={{0,12},{4,0},{8,4},{12,8},{1,13},{5,1},{9,5},{13,9},{2,14},{6,2},{... | collective-permute-start | bytes 1179656 | tf_op jit(solution)/shard_map/ppermute | solution.py:402
  101.1 17.7 %collective-permute-start.16 = (bf16[256,768]{1,0:T(8,128)(2,1)S(1)}, bf16[256,768]{1,0:T(8,128)(2,1)S(1)}, u32[]{:S(2)}, u32[]{:S(2)}) collective-permute-start(bf16[256,768]{1,0:T(8,128)(2,1)S(1)} %get-tuple-element.61), channel_id=1, source_target_pairs={{0,8},{4,12},{8,0},{12,4},{1,9},{5,13},{9,1},{13,5},{2,10},{6,14},... | collective-permute-start | bytes 1179656 | tf_op jit(solution)/shard_map/ppermute | solution.py:402
  121.1 6.0 %collective-permute-start.17 = (bf16[144,768]{1,0:T(8,128)(2,1)S(1)}, bf16[144,768]{1,0:T(8,128)(2,1)S(1)}, u32[]{:S(2)}, u32[]{:S(2)}) collective-permute-start(bf16[144,768]{1,0:T(8,128)(2,1)S(1)} %get-tuple-element.75), channel_id=1, source_target_pairs={{0,16},{16,0},{1,17},{17,1},{2,18},{18,2},{3,19},{19,3},{4,20},{20... | collective-permute-start | bytes 663560 | tf_op jit(solution)/shard_map/ppermute | solution.py:397
  146.3 9.8 %collective-permute-start.18 = (f32[48,192]{1,0:T(8,128)S(1)}, f32[48,192]{1,0:T(8,128)S(1)}, u32[]{:S(2)}, u32[]{:S(2)}) collective-permute-start(f32[48,192]{1,0:T(8,128)S(1)} %get-tuple-element.78), channel_id=1, source_target_pairs={{0,0},{1,64},{2,128},{3,192},{32,1},{33,65},{34,129},{35,193},{64,... | collective-permute-start | bytes 110600 | tf_op jit(solution)/shard_map/ppermute | solution.py:450

commit v2 on v1

--- a/solution.py
+++ b/solution.py
@@ -178,6 +178,70 @@
 
 def factor_sum_z(messages):
     return call(factor_sum_z_kernel, "factor_sum_z", shape(TILE, dtype=f32), [VMEM])(messages)
+
+
+def factor_parts(own, same, other, p):
+    peak = jnp.zeros((1, 1), f32)
+    for b, rows in enumerate((same, other)):
+        for c in range(3):
+            cols = slice(c * 256, (c + 1) * 256)
+            tile = crossed(rows[...], own[:, cols]) * (1.0 / ROWS)
+            p[b, :, cols] = tile
+            peak = peak_of(tile, peak)
+    return exponent_of(peak)
+
+
+def near_kernel(idx, own, same, other, out, p):
+    core = idx[4]
+    e = factor_parts(own, same, other, p)
+    scale = scale_of(e)
+    for b, slot in enumerate((core, 1 - core)):
+        for hyx in range(16):
+            dst = pl.multiple_of((slot * 4 + hyx // 4) * TILE, TILE)
+            src = slice(hyx * TILE, (hyx + 1) * TILE)
+            out[hyx % 4, pl.ds(dst, TILE), :] = coded(p[b, src, :] * scale).astype(bf16)
+    for x in range(4):
+        out[x, 8 * TILE :, :] = spread(e, PAD, BLOCK).astype(bf16)
+
+
+def near_messages(idx, own, same, other):
+    return call(
+        near_kernel,
+        "near",
+        jax.ShapeDtypeStruct((4, 8 * TILE + PAD, BLOCK), bf16),
+        [SMEM] + [VMEM] * 3,
+        [pltpu.VMEM((2, BLOCK, BLOCK), f32)],
+    )(idx, own, same, other)
+
+
+def near_sum_x_kernel(idx, m, send, keep, held):
+    yl = idx[1]
+    factors = [unscale_of(m[d, 8 * TILE :, 0:128]) for d in range(4)]
+
+    def total(b, y):
+        rows = pl.ds(pl.multiple_of((b * 2 + y) * TILE, TILE), TILE)
+        parts = [decoded(m[d, rows, :]) * factors[d] for d in range(4)]
+        return (parts[0] + parts[1]) + (parts[2] + parts[3])
+
+    peak = jnp.zeros((1, 1), f32)
+    for b in range(4):
+        keep[b * TILE : (b + 1) * TILE, :] = total(b, yl)
+        out = total(b, 1 - yl)
+        held[b * TILE : (b + 1) * TILE, :] = out
+        peak = peak_of(out, peak)
+    e = exponent_of(peak)
+    send[0 : 4 * TILE, :] = coded(held[...] * scale_of(e)).astype(bf16)
+    send[4 * TILE :, :] = spread(e, PAD, BLOCK).astype(bf16)
+
+
+def near_sum_x(idx, messages):
+    return call(
+        near_sum_x_kernel,
+        "near_sum_x",
+        [shape(4 * TILE + PAD), shape(4 * TILE, dtype=f32)],
+        [SMEM, VMEM],
+        [pltpu.VMEM((4 * TILE, BLOCK), f32)],
+    )(idx, messages)
 
 
 def proj_kernel(first, idx, a, b, basis, *rest):
@@ -418,28 +482,28 @@
     both = side_by_side(activations, basis_act)
     both_other = swap(both, "core")
 
-    msg_a = factor_messages(idx, gradients, gradients, grad_other)
-    got_a = along_x(msg_a)
-    proj = project(idx, (0, 0), after(gradients, both_other, *msg_a), grad_other, basis_grad, None, f32)
+    msg_near = near_messages(idx, gradients, gradients, grad_other)
+    near_x = lax.all_to_all(msg_near, "x", 0, 0)
+    proj = project(idx, (0, 0), after(gradients, both_other, msg_near), grad_other, basis_grad, None, f32)
 
     grad_far, proj = lax.optimization_barrier((grad_far, proj))
-    grad_far_other = swap(after(grad_far, *got_a[1:3]), "core")
+    grad_far_other = swap(grad_far, "core")
     both_far = swap(after(both, grad_far), "yh")
     msg_b = factor_messages(idx, gradients, grad_far, grad_far_other)
-    proj, *got_a = lax.optimization_barrier((proj,) + tuple(got_a) + tuple(msg_b))[:5]
     got_b = along_x(msg_b)
+    send_a, keep_a = near_sum_x(idx, after(near_x, *msg_b))
+    proj, both_far = lax.optimization_barrier((proj, both_far, send_a))[:2]
+    both_far_other = swap(both_far, "core")
     proj_grad = project(idx, (2, 0), grad_far, grad_far_other, basis_grad, proj, bf16)
-    both_far_other = swap(after(both_far, proj_grad), "core")
 
     proj_act, act = act_parts(idx, (both, both_other, both_far, both_far_other))
     msg_e = scales_messages(idx, proj_grad, proj_act, act)
     got_e = along_x(msg_e)
 
-    send_a, keep_a = factor_sum_x(idx, [after(got_a[0], *msg_e)] + list(got_a[1:]))
     y_a = swap(send_a, "yl")
-    send_b, keep_b = factor_sum_x(idx, [after(got_b[0], send_a)] + got_b[1:])
+    send_b, keep_b = factor_sum_x(idx, [after(got_b[0], *msg_e)] + got_b[1:])
     y_b = swap(send_b, "yl")
-    to_z = factor_sum_y(idx, keep_a, y_a, keep_b, y_b)
+    to_z = factor_sum_y(idx, keep_a, after(y_a, *got_e), keep_b, y_b)
     z_cov = lax.all_to_all(to_z, "z", 0, 0)
     grad_factor = factor_sum_z(z_cov)
 

time: 157 us -> 160 us (1.019)
  local copies, waits for them, and re-layouts: 5.31 us -> 11.7 us
  waiting for transfers between devices: 63.1 us -> 58.3 us
  blocking collectives: 17.2 us -> 14.7 us
  Pallas kernels: 41.2 us -> 43 us
    ppermute x9, waiting for transfers between devices: 27.9 us -> 13.7 us  [swap(): return lax.ppermute(value, axis, [(0, 1), (1, 0)])]
    all_to_all x1, waiting for transfers between devices: 0.01 us -> 12.8 us  [on_device(): z_cov = lax.all_to_all(to_z, 'z', 0, 0)]
    pallas_call x0 -> x2, Pallas kernels: none -> 10.9 us  [the longest x1 6.21 us: near_messages(): call(near_kernel, 'near', jax.ShapeDtypeStruct((4, 8 * TILE + PAD, BLOCK)...]
    unnamed x23 -> x37, local copies, waits for them, and re-layouts: 5.23 us -> 11.6 us
    ppermute x9 -> x6, waiting for transfers between devices: 29.8 us -> 23.8 us  [along_x(): lax.ppermute(messages[d], 'x', [(i, (i + d) % 4) for i in range(4)])]
    pallas_call x2 -> x1, Pallas kernels: 10.9 us -> 5.39 us  [factor_messages(): call(factor_kernel, 'factor', [shape(8 * TILE + PAD)] * 4, [SMEM] + [VMEM...]
    all_to_all x0 -> x1, starting transfers between devices: none -> 5.15 us  [on_device(): near_x = lax.all_to_all(msg_near, 'x', 0, 0)]
    pallas_call x2 -> x1, Pallas kernels: 7.48 us -> 3.38 us  [factor_sum_x(): call(factor_sum_x_kernel, 'factor_sum_x', [shape(4 * TILE + PAD), shape(4...]
  transfers between devices with their start and end apart: 20 -> 18, of which waited for: 12 -> 11; matrix products, arithmetic and copies ran while one was open for 0% -> 1% of each run, Pallas kernels for 24% -> 25%
where the time goes in v2:
time: 160 us; the launch traced here: 159 us
  waiting for transfers between devices  58.3 us (36%)
  Pallas kernels  43 us (27%)
  starting transfers between devices  30.7 us (19%)
  blocking collectives  14.7 us (9%)
  local copies, waits for them, and re-layouts  11.7 us (7%)
    ppermute x6, waiting for transfers between devices, along_x(): lax.ppermute(messages[d], 'x', [(i, (i + d) % 4) for i in range(4)])  23.8 us
    all_to_all x1, blocking collectives, on_device(): lax.all_to_all(after(scales_sum_y(idx, keep_e, keep_act, y_e), z_cov), 'z...  14.7 us
    ppermute x9, waiting for transfers between devices, swap(): return lax.ppermute(value, axis, [(0, 1), (1, 0)])  13.7 us
    all_to_all x1, waiting for transfers between devices, on_device(): z_cov = lax.all_to_all(to_z, 'z', 0, 0)  12.8 us
    unnamed x37, local copies, waits for them, and re-layouts  11.6 us
    pallas_call x2, Pallas kernels, project(): call(functools.partial(proj_kernel, first), 'project', shape(HW, dtype=dt...  8.84 us
    all_to_all x1, starting transfers between devices, on_device(): z_cov = lax.all_to_all(to_z, 'z', 0, 0)  8.47 us
    ppermute x6, starting transfers between devices, along_x(): lax.ppermute(messages[d], 'x', [(i, (i + d) % 4) for i in range(4)])  8.43 us
  transfers between devices with their start and end apart: 18, of which 11 were waited for; matrix products, arithmetic and copies ran while one was open for 1% of the time, Pallas kernels for 25%

profile of v2, /device:TPU:26, one launch (start us, length us, event | category | flops | bytes accessed | tf_op | source)
XLA Modules:
  0.0 159.2 jit_solution(12983667598208807453)
XLA Ops:
  0.7 1.3 collective-permute-start
  2.1 1.7 %collective-permute-done.2.other.b = bf16[784,768]{1,0:T(8,128)(2,1)S(1)} collective-permute-done((bf16[784,768]{1,0:T(8,128)(2,1)}, bf16[784,768]{1,0:T(8,128)(2,1)S(1)}, u32[]{:S(2)}, u32[]{:S(2)}) %collective-permute-start.2) | collective-permute-done | bytes 1204256 | tf_op jit(solution)/shard_map/ppermute | solution.py:461
  3.8 1.3 copy-done
  5.1 6.2 %near.1 = bf16[4,400,768]{2,1,0:T(8,128)(2,1)} custom-call(s32[5]{0:T(128)S(1)} %stack.23.idx, bf16[784,768]{1,0:T(8,128)(2,1)S(1)} %copy-done, bf16[784,768]{1,0:T(8,128)(2,1)S(1)} %copy-done, bf16[784,768]{1,0:T(8,128)(2,1)S(1)} %collective-permute-done.2.other.b), custom_call_target="tpu_custom_call" | custom-call | flops 1 | bytes 1 | tf_op jit(solution)/shard_map/near/pallas_call | solution.py:208
  11.3 5.1 %all-to-all-start = ((bf16[4,400,768]{2,1,0:T(8,128)(2,1)}), bf16[4,400,768]{2,1,0:T(8,128)(2,1)}, u32[]{:S(2)}, u32[]{:S(2)}) async-start(bf16[4,400,768]{2,1,0:T(8,128)(2,1)} %near.1), calls=%async_computation | async-start | bytes 4915200 | tf_op jit(solution)/shard_map/all_to_all | solution.py:486
  16.5 0.9 copy.8.basis
  17.6 1.1 copy-done.8
  19.0 2.0 %collective-permute-done.1.b1 = bf16[784,384]{1,0:T(8,128)(2,1)S(1)} collective-permute-done((bf16[784,384]{1,0:T(8,128)(2,1)S(1)}, bf16[784,384]{1,0:T(8,128)(2,1)S(1)}, u32[]{:S(2)}, u32[]{:S(2)}) %collective-permute-start.1) | collective-permute-done | bytes 602144 | tf_op jit(solution)/shard_map/ppermute | solution.py:461
  21.0 0.8 copy-done.11
  21.8 1.3 copy-done.5
  23.1 4.4 %project.2.rest_0_ = f32[784,768]{1,0:T(8,128)S(1)} custom-call(s32[5]{0:T(128)S(1)} %stack.23.idx, bf16[784,768]{1,0:T(8,128)(2,1)S(1)} %copy-done.1, bf16[784,768]{1,0:T(8,128)(2,1)S(1)} %copy-done.5, bf16[3072,768]{1,0:T(8,128)(2,1)} %basis.4), custom_call_target="tpu_custom_call" | custom-call | flops 1 | bytes 1 | tf_op jit(solution)/shard_map/project/pallas_call | solution.py:264
  27.5 1.5 copy-done.2
  29.0 2.4 %collective-permute-done.same.a = bf16[784,768]{1,0:T(8,128)(2,1)S(1)} collective-permute-done((bf16[784,768]{1,0:T(8,128)(2,1)}, bf16[784,768]{1,0:T(8,128)(2,1)S(1)}, u32[]{:S(2)}, u32[]{:S(2)}) %collective-permute-start) | collective-permute-done | bytes 1204256 | tf_op jit(solution)/shard_map/ppermute | solution.py:461
  31.4 1.2 collective-permute-start.4
  32.6 1.6 %collective-permute-done.3.other.b = bf16[784,768]{1,0:T(8,128)(2,1)S(1)} collective-permute-done((bf16[784,768]{1,0:T(8,128)(2,1)S(1)}, bf16[784,768]{1,0:T(8,128)(2,1)S(1)}, u32[]{:S(2)}, u32[]{:S(2)}) %collective-permute-start.3) | collective-permute-done | bytes 1204256 | tf_op jit(solution)/shard_map/ppermute | solution.py:461
  34.2 5.4 %factor.1 = (bf16[400,768]{1,0:T(8,128)(2,1)S(1)}, bf16[400,768]{1,0:T(8,128)(2,1)}, bf16[400,768]{1,0:T(8,128)(2,1)S(1)}, bf16[400,768]{1,0:T(8,128)(2,1)S(1)}) custom-call(s32[5]{0:T(128)S(1)} %stack.23.idx, bf16[784,768]{1,0:T(8,128)(2,1)S(1)} %copy-done.1, bf16[784,768]{1,0:T(8,128)(2,1)S(1)} %collective-permute-done.same.a, ...), custom_call_target="tpu_custom_call" | custom-call | flops 1 | bytes 1 | tf_op jit(solution)/shard_map/factor/pallas_call | solution.py:106
  39.6 0.8 copy-done.9
  40.5 0.9 copy-done.13
  41.3 0.8 copy-done.14
  42.2 1.5 collective-permute-start.10
  43.7 2.2 %all-to-all-done.m = bf16[4,400,768]{2,1,0:T(8,128)(2,1)} async-done(((bf16[4,400,768]{2,1,0:T(8,128)(2,1)}), bf16[4,400,768]{2,1,0:T(8,128)(2,1)}, u32[]{:S(2)}, u32[]{:S(2)}) %all-to-all-start) | async-done | bytes 2457632 | tf_op jit(solution)/shard_map/all_to_all | solution.py:486
  45.9 4.7 %near_sum_x.1 = (bf16[208,768]{1,0:T(8,128)(2,1)S(1)}, f32[192,768]{1,0:T(8,128)S(1)}) custom-call(s32[5]{0:T(128)S(1)} %stack.23.idx, bf16[4,400,768]{2,1,0:T(8,128)(2,1)} %all-to-all-done.m), custom_call_target="tpu_custom_call" | custom-call | flops 1 | bytes 1 | tf_op jit(solution)/shard_map/near_sum_x/pallas_call | solution.py:238
  50.7 1.5 collective-permute-start.12
  52.8 1.3 copy-done.7
  54.1 4.5 %project.3.pg = bf16[784,768]{1,0:T(8,128)(2,1)S(1)} custom-call(s32[5]{0:T(128)S(1)} %stack.23.idx, bf16[784,768]{1,0:T(8,128)(2,1)S(1)} %collective-permute-done.same.a, bf16[784,768]{1,0:T(8,128)(2,1)S(1)} %copy-done.7, bf16[3072,768]{1,0:T(8,128)(2,1)} %basis.4, f32[784,768]{1,0:T(8,128)S(1)} %copy-done.3), custom_call_target="tpu_custom_call" | custom-call | flops 1 | bytes 1 | tf_op jit(solution)/shard_map/project/pallas_call | solution.py:264
  58.6 3.4 %act.2 = (bf16[784,768]{1,0:T(8,128)(2,1)S(1)}, f32[4,48,768]{2,1,0:T(8,128)S(1)}) custom-call(s32[5]{0:T(128)S(1)} %stack.23.idx, bf16[784,384]{1,0:T(8,128)(2,1)S(1)} %beside.1.b0, bf16[784,384]{1,0:T(8,128)(2,1)S(1)} %copy-done.12, bf16[784,384]{1,0:T(8,128)(2,1)} %collective-permute-done.4.b2, bf16[784,384]{1,0:T(8,128)(2,1)S(1)} %collective-permute-done.5.b3), custom_call_target="tpu_custom_call" | custom-call | flops 1 | bytes 1 | tf_op jit(solution)/shard_map/act/pallas_call | solution.py:313
  62.0 2.9 %scales.1 = (bf16[256,768]{1,0:T(8,128)(2,1)S(1)}, bf16[256,768]{1,0:T(8,128)(2,1)S(1)}, bf16[256,768]{1,0:T(8,128)(2,1)S(1)}, bf16[256,768]{1,0:T(8,128)(2,1)S(1)}) custom-call(s32[5]{0:T(128)S(1)} %stack.23.idx, bf16[784,768]{1,0:T(8,128)(2,1)S(1)} %project.3.pg, bf16[784,768]{1,0:T(8,128)(2,1)S(1)} %get-tuple-element.45.pa, ...), custom_call_target="tpu_custom_call" | custom-call | flops 1 | bytes 1 | tf_op jit(solution)/shard_map/scales/pallas_call | solution.py:352
  64.9 1.5 collective-permute-start.7
  66.4 1.3 collective-permute-start.8
  67.7 2.0 %collective-permute-start.9 = (bf16[256,768]{1,0:T(8,128)(2,1)S(1)}, bf16[256,768]{1,0:T(8,128)(2,1)S(1)}, u32[]{:S(2)}, u32[]{:S(2)}) collective-permute-start(bf16[256,768]{1,0:T(8,128)(2,1)S(1)} %get-tuple-element.51), channel_id=1, source_target_pairs={{0,8},{4,12},{8,0},{12,4},{1,9},{5,13},{9,1},{13,5},{2,10},{6,14},... | collective-permute-start | bytes 1179656 | tf_op jit(solution)/shard_map/ppermute | solution.py:466
  69.7 0.7 collective-permute-start.6
  70.5 11.4 %collective-permute-done.11.m2 = bf16[400,768]{1,0:T(8,128)(2,1)S(1)} collective-permute-done((bf16[400,768]{1,0:T(8,128)(2,1)}, bf16[400,768]{1,0:T(8,128)(2,1)S(1)}, u32[]{:S(2)}, u32[]{:S(2)}) %collective-permute-start.11) | collective-permute-done | bytes 614432 | tf_op jit(solution)/shard_map/ppermute | solution.py:466
  81.9 3.4 %factor_sum_x.1 = (bf16[208,768]{1,0:T(8,128)(2,1)S(1)}, f32[192,768]{1,0:T(8,128)S(1)}) custom-call(s32[5]{0:T(128)S(1)} %stack.23.idx, bf16[400,768]{1,0:T(8,128)(2,1)S(1)} %copy-done.10, bf16[400,768]{1,0:T(8,128)(2,1)S(1)} %collective-permute-done.10.m1, bf16[400,768]{1,0:T(8,128)(2,1)S(1)} %collective-permute-done.11.m2, ...), custom_call_target="tpu_custom_call" | custom-call | flops 1 | bytes 1 | tf_op jit(solution)/shard_map/factor_sum_x/pallas_call | solution.py:136
  85.3 1.1 collective-permute-start.13
  86.4 3.6 %collective-permute-done.8.m2 = bf16[256,768]{1,0:T(8,128)(2,1)S(1)} collective-permute-done((bf16[256,768]{1,0:T(8,128)(2,1)S(1)}, bf16[256,768]{1,0:T(8,128)(2,1)S(1)}, u32[]{:S(2)}, u32[]{:S(2)}) %collective-permute-start.8) | collective-permute-done | bytes 393248 | tf_op jit(solution)/shard_map/ppermute | solution.py:466
  90.0 8.7 %collective-permute-done.9.m3 = bf16[256,768]{1,0:T(8,128)(2,1)S(1)} collective-permute-done((bf16[256,768]{1,0:T(8,128)(2,1)S(1)}, bf16[256,768]{1,0:T(8,128)(2,1)S(1)}, u32[]{:S(2)}, u32[]{:S(2)}) %collective-permute-start.9) | collective-permute-done | bytes 393248 | tf_op jit(solution)/shard_map/ppermute | solution.py:466
  98.7 2.5 %factor_sum_y.1 = bf16[8,64,768]{2,1,0:T(8,128)(2,1)} custom-call(s32[5]{0:T(128)S(1)} %stack.23.idx, f32[192,768]{1,0:T(8,128)S(1)} %get-tuple-element.48.keep_a, bf16[208,768]{1,0:T(8,128)(2,1)S(1)} %collective-permute-done.6.got_a, f32[192,768]{1,0:T(8,128)S(1)} %get-tuple-element.54.keep_b, bf16[208,768]{1,0:T(8,128)(2,1)S(1)} %collective-permute-done.13.got_b), custom_call_target="tpu_custom_call" | custom-call | flops 1 | bytes 1 | tf_op jit(solution)/shard_map/factor_sum_y/pallas_call | solution.py:163
  101.3 8.5 %all-to-all-start.1 = ((bf16[8,64,768]{2,1,0:T(8,128)(2,1)}), bf16[8,64,768]{2,1,0:T(8,128)(2,1)S(1)}, u32[]{:S(2)}, u32[]{:S(2)}) async-start(bf16[8,64,768]{2,1,0:T(8,128)(2,1)} %factor_sum_y.1), calls=%async_computation.1 | async-start | bytes 1572864 | tf_op jit(solution)/shard_map/all_to_all | solution.py:507
  109.7 2.3 %scales_sum_x.1 = (bf16[144,768]{1,0:T(8,128)(2,1)S(1)}, f32[96,768]{1,0:T(8,128)S(1)}, f32[24,768]{1,0:T(8,128)S(1)}) custom-call(s32[5]{0:T(128)S(1)} %stack.23.idx, bf16[256,768]{1,0:T(8,128)(2,1)S(1)} %get-tuple-element.56.m0, bf16[256,768]{1,0:T(8,128)(2,1)S(1)} %collective-permute-done.7.m1, bf16[256,768]{1,0:T(8,128)(2,1)S(1)} %collective-permute-done.8.m2, ...), custom_call_target="tpu_custom_call" | custom-call | flops 1 | bytes 1 | tf_op jit(solution)/shard_map/scales_sum_x/pallas_call | solution.py:395
  112.0 0.8 collective-permute-start.14
  112.9 5.9 %collective-permute-done.14.got = bf16[144,768]{1,0:T(8,128)(2,1)S(1)} collective-permute-done((bf16[144,768]{1,0:T(8,128)(2,1)S(1)}, bf16[144,768]{1,0:T(8,128)(2,1)S(1)}, u32[]{:S(2)}, u32[]{:S(2)}) %collective-permute-start.14) | collective-permute-done | bytes 221216 | tf_op jit(solution)/shard_map/ppermute | solution.py:461
  118.8 1.0 scales_sum_y.1
  119.8 12.8 %all-to-all-done.1.m = bf16[8,64,768]{2,1,0:T(8,128)(2,1)S(1)} async-done(((bf16[8,64,768]{2,1,0:T(8,128)(2,1)}), bf16[8,64,768]{2,1,0:T(8,128)(2,1)S(1)}, u32[]{:S(2)}, u32[]{:S(2)}) %all-to-all-start.1) | async-done | bytes 786464 | tf_op jit(solution)/shard_map/all_to_all | solution.py:507
  132.6 14.7 %all_to_all.15.m = bf16[8,64,192]{2,1,0:T(8,128)(2,1)S(1)} all-to-all(bf16[8,64,192]{2,1,0:T(8,128)(2,1)S(1)} %scales_sum_y.1), channel_id=1, replica_groups=mesh['z'=8,'yl'=2,'x'=4,'yh'=2,'core'=2] {'z'}, dimensions={0} | all-to-all | bytes 393216 | tf_op jit(solution)/shard_map/all_to_all | solution.py:512
  147.4 0.9 scales_sum_z.1
  148.2 3.1 %collective-permute-start.15 = (f32[48,192]{1,0:T(8,128)S(1)}, f32[48,192]{1,0:T(8,128)S(1)}, u32[]{:S(2)}, u32[]{:S(2)}) collective-permute-start(f32[48,192]{1,0:T(8,128)S(1)} %get-tuple-element.62), channel_id=1, source_target_pairs={{0,0},{1,64},{2,128},{3,192},{32,1},{33,65},{34,129},{35,193},{64,... | collective-permute-start | bytes 110600 | tf_op jit(solution)/shard_map/ppermute | solution.py:514
  151.4 1.3 factor_sum_z.1
  152.7 5.9 %collective-permute-done.15 = f32[48,192]{1,0:T(8,128)S(1)} collective-permute-done((f32[48,192]{1,0:T(8,128)S(1)}, f32[48,192]{1,0:T(8,128)S(1)}, u32[]{:S(2)}, u32[]{:S(2)}) %collective-permute-start.15) | collective-permute-done | bytes 36896 | tf_op jit(solution)/shard_map/ppermute | solution.py:514
  (41 shorter events, 2.0 us)
Async XLA Ops:
  0.6 3.2 %collective-permute-start.2 = (bf16[784,768]{1,0:T(8,128)(2,1)}, bf16[784,768]{1,0:T(8,128)(2,1)S(1)}, u32[]{:S(2)}, u32[]{:S(2)}) collective-permute-start(bf16[784,768]{1,0:T(8,128)(2,1)} %own.3), channel_id=1, source_target_pairs={{0,1},{1,0},{2,3},{3,2},{4,5},{5,4},{6,7},{7,6},{8,9},{9,8},{10,11... | collective-permute-start | bytes 3612680 | tf_op jit(solution)/shard_map/ppermute | solution.py:461
  0.7 30.6 %collective-permute-start = (bf16[784,768]{1,0:T(8,128)(2,1)}, bf16[784,768]{1,0:T(8,128)(2,1)S(1)}, u32[]{:S(2)}, u32[]{:S(2)}) collective-permute-start(bf16[784,768]{1,0:T(8,128)(2,1)} %own.3), channel_id=1, source_target_pairs={{0,2},{2,0},{1,3},{3,1},{4,6},{6,4},{5,7},{7,5},{8,10},{10,8},{9,1... | collective-permute-start | bytes 3612680 | tf_op jit(solution)/shard_map/ppermute | solution.py:461
  3.8 1.3 copy-start
  5.1 6.2 %copy-start.4 = (bf16[784,768]{1,0:T(8,128)(2,1)}, bf16[784,768]{1,0:T(8,128)(2,1)S(1)}, u32[]{:S(2)}) copy-start(bf16[784,768]{1,0:T(8,128)(2,1)S(1)} %collective-permute-done.2.other.b) | copy-start | bytes 3612676
  11.3 5.2 %copy-start.16 = (bf16[768,192]{0,1:T(8,128)(2,1)S(1)}, bf16[768,192]{0,1:T(8,128)(2,1)}, u32[]{:S(2)}) copy-start(bf16[768,192]{0,1:T(8,128)(2,1)} %param.6) | copy-start | bytes 884740
  11.3 6.1 %copy-start.15 = (bf16[784,192]{0,1:T(8,128)(2,1)S(1)}, bf16[784,192]{0,1:T(8,128)(2,1)}, u32[]{:S(2)}) copy-start(bf16[784,192]{0,1:T(8,128)(2,1)} %param.4) | copy-start | bytes 903172
  11.3 34.6 %all-to-all-start = ((bf16[4,400,768]{2,1,0:T(8,128)(2,1)}), bf16[4,400,768]{2,1,0:T(8,128)(2,1)}, u32[]{:S(2)}, u32[]{:S(2)}) async-start(bf16[4,400,768]{2,1,0:T(8,128)(2,1)} %near.1), calls=%async_computation | async-start | bytes 4915200 | tf_op jit(solution)/shard_map/all_to_all | solution.py:486
  17.4 4.4 %copy-start.1 = (bf16[784,768]{1,0:T(8,128)(2,1)S(1)}, bf16[784,768]{1,0:T(8,128)(2,1)}, u32[]{:S(2)}) copy-start(bf16[784,768]{1,0:T(8,128)(2,1)} %own.3) | copy-start | bytes 3612676
  17.6 1.1 copy-start.8
  18.9 2.1 %collective-permute-start.1 = (bf16[784,384]{1,0:T(8,128)(2,1)S(1)}, bf16[784,384]{1,0:T(8,128)(2,1)S(1)}, u32[]{:S(2)}, u32[]{:S(2)}) collective-permute-start(bf16[784,384]{1,0:T(8,128)(2,1)S(1)} %beside.1.b0), channel_id=1, source_target_pairs={{0,1},{1,0},{2,3},{3,2},{4,5},{5,4},{6,7},{7,6},{8,9},{9,8},{10,11... | collective-permute-start | bytes 1806344 | tf_op jit(solution)/shard_map/ppermute | solution.py:461
  21.0 0.8 copy-start.11
  21.8 1.3 copy-start.5
  27.5 1.5 copy-start.2
  31.4 2.9 %collective-permute-start.3 = (bf16[784,768]{1,0:T(8,128)(2,1)S(1)}, bf16[784,768]{1,0:T(8,128)(2,1)S(1)}, u32[]{:S(2)}, u32[]{:S(2)}) collective-permute-start(bf16[784,768]{1,0:T(8,128)(2,1)S(1)} %collective-permute-done.same.a), channel_id=1, source_target_pairs={{0,1},{1,0},{2,3},{3,2},{4,5},{5,4},{6,7},{7,6},{8,9},{9,8},{10,11... | collective-permute-start | bytes 3612680 | tf_op jit(solution)/shard_map/ppermute | solution.py:461
  31.4 19.2 %collective-permute-start.4 = (bf16[784,384]{1,0:T(8,128)(2,1)S(1)}, bf16[784,384]{1,0:T(8,128)(2,1)}, u32[]{:S(2)}, u32[]{:S(2)}) collective-permute-start(bf16[784,384]{1,0:T(8,128)(2,1)S(1)} %beside.1.b0), channel_id=1, source_target_pairs={{0,2},{2,0},{1,3},{3,1},{4,6},{6,4},{5,7},{7,5},{8,10},{10,8},{9,1... | collective-permute-start | bytes 1806344 | tf_op jit(solution)/shard_map/ppermute | solution.py:461
  34.2 5.4 %copy-start.6 = (bf16[784,768]{1,0:T(8,128)(2,1)}, bf16[784,768]{1,0:T(8,128)(2,1)S(1)}, u32[]{:S(2)}) copy-start(bf16[784,768]{1,0:T(8,128)(2,1)S(1)} %collective-permute-done.3.other.b) | copy-start | bytes 3612676
  39.6 0.8 copy-start.9
  40.5 0.9 copy-start.13
  41.3 0.8 copy-start.14
  42.2 25.6 %collective-permute-start.10 = (bf16[400,768]{1,0:T(8,128)(2,1)}, bf16[400,768]{1,0:T(8,128)(2,1)S(1)}, u32[]{:S(2)}, u32[]{:S(2)}) collective-permute-start(bf16[400,768]{1,0:T(8,128)(2,1)} %get-tuple-element.38), channel_id=1, source_target_pairs={{0,4},{4,8},{8,12},{12,0},{1,5},{5,9},{9,13},{13,1},{2,6},{6,10},{... | collective-permute-start | bytes 1843208 | tf_op jit(solution)/shard_map/ppermute | solution.py:466
  45.9 6.9 %copy-start.3 = (f32[784,768]{1,0:T(8,128)S(1)}, f32[784,768]{1,0:T(8,128)}, u32[]{:S(2)}) copy-start(f32[784,768]{1,0:T(8,128)} %copy-done.2) | copy-start | bytes 7225348
  50.6 8.0 %collective-permute-start.5 = (bf16[784,384]{1,0:T(8,128)(2,1)}, bf16[784,384]{1,0:T(8,128)(2,1)S(1)}, u32[]{:S(2)}, u32[]{:S(2)}) collective-permute-start(bf16[784,384]{1,0:T(8,128)(2,1)} %collective-permute-done.4.b2), channel_id=1, source_target_pairs={{0,1},{1,0},{2,3},{3,2},{4,5},{5,4},{6,7},{7,6},{8,9},{9,8},{10,11... | collective-permute-start | bytes 1806344 | tf_op jit(solution)/shard_map/ppermute | solution.py:461
  50.7 19.1 %collective-permute-start.12 = (bf16[400,768]{1,0:T(8,128)(2,1)}, bf16[400,768]{1,0:T(8,128)(2,1)S(1)}, u32[]{:S(2)}, u32[]{:S(2)}) collective-permute-start(bf16[400,768]{1,0:T(8,128)(2,1)} %copy-done.14), channel_id=1, source_target_pairs={{0,8},{4,12},{8,0},{12,4},{1,9},{5,13},{9,1},{13,5},{2,10},{6,14},... | collective-permute-start | bytes 1843208 | tf_op jit(solution)/shard_map/ppermute | solution.py:466
  52.2 29.7 %collective-permute-start.11 = (bf16[400,768]{1,0:T(8,128)(2,1)}, bf16[400,768]{1,0:T(8,128)(2,1)S(1)}, u32[]{:S(2)}, u32[]{:S(2)}) collective-permute-start(bf16[400,768]{1,0:T(8,128)(2,1)} %copy-done.13), channel_id=1, source_target_pairs={{0,12},{4,0},{8,4},{12,8},{1,13},{5,1},{9,5},{13,9},{2,14},{6,2},{... | collective-permute-start | bytes 1843208 | tf_op jit(solution)/shard_map/ppermute | solution.py:466
  52.8 1.3 copy-start.7
  54.1 4.5 %copy-start.12 = (bf16[784,384]{1,0:T(8,128)(2,1)S(1)}, bf16[784,384]{1,0:T(8,128)(2,1)}, u32[]{:S(2)}) copy-start(bf16[784,384]{1,0:T(8,128)(2,1)} %copy-done.11) | copy-start | bytes 1806340
  62.0 19.9 %copy-start.10 = (bf16[400,768]{1,0:T(8,128)(2,1)S(1)}, bf16[400,768]{1,0:T(8,128)(2,1)}, u32[]{:S(2)}) copy-start(bf16[400,768]{1,0:T(8,128)(2,1)} %copy-done.9) | copy-start | bytes 1843204
  64.9 21.5 %collective-permute-start.7 = (bf16[256,768]{1,0:T(8,128)(2,1)S(1)}, bf16[256,768]{1,0:T(8,128)(2,1)S(1)}, u32[]{:S(2)}, u32[]{:S(2)}) collective-permute-start(bf16[256,768]{1,0:T(8,128)(2,1)S(1)} %get-tuple-element.49), channel_id=1, source_target_pairs={{0,4},{4,8},{8,12},{12,0},{1,5},{5,9},{9,13},{13,1},{2,6},{6,10},{... | collective-permute-start | bytes 1179656 | tf_op jit(solution)/shard_map/ppermute | solution.py:466
  66.4 23.6 %collective-permute-start.8 = (bf16[256,768]{1,0:T(8,128)(2,1)S(1)}, bf16[256,768]{1,0:T(8,128)(2,1)S(1)}, u32[]{:S(2)}, u32[]{:S(2)}) collective-permute-start(bf16[256,768]{1,0:T(8,128)(2,1)S(1)} %get-tuple-element.50), channel_id=1, source_target_pairs={{0,12},{4,0},{8,4},{12,8},{1,13},{5,1},{9,5},{13,9},{2,14},{6,2},{... | collective-permute-start | bytes 1179656 | tf_op jit(solution)/shard_map/ppermute | solution.py:466
  67.7 31.0 %collective-permute-start.9 = (bf16[256,768]{1,0:T(8,128)(2,1)S(1)}, bf16[256,768]{1,0:T(8,128)(2,1)S(1)}, u32[]{:S(2)}, u32[]{:S(2)}) collective-permute-start(bf16[256,768]{1,0:T(8,128)(2,1)S(1)} %get-tuple-element.51), channel_id=1, source_target_pairs={{0,8},{4,12},{8,0},{12,4},{1,9},{5,13},{9,1},{13,5},{2,10},{6,14},... | collective-permute-start | bytes 1179656 | tf_op jit(solution)/shard_map/ppermute | solution.py:466
  69.7 16.7 %collective-permute-start.6 = (bf16[208,768]{1,0:T(8,128)(2,1)S(1)}, bf16[208,768]{1,0:T(8,128)(2,1)S(1)}, u32[]{:S(2)}, u32[]{:S(2)}) collective-permute-start(bf16[208,768]{1,0:T(8,128)(2,1)S(1)} %get-tuple-element.42), channel_id=1, source_target_pairs={{0,16},{16,0},{1,17},{17,1},{2,18},{18,2},{3,19},{19,3},{4,20},{20... | collective-permute-start | bytes 958472 | tf_op jit(solution)/shard_map/ppermute | solution.py:461
  85.3 13.4 %collective-permute-start.13 = (bf16[208,768]{1,0:T(8,128)(2,1)S(1)}, bf16[208,768]{1,0:T(8,128)(2,1)S(1)}, u32[]{:S(2)}, u32[]{:S(2)}) collective-permute-start(bf16[208,768]{1,0:T(8,128)(2,1)S(1)} %get-tuple-element.55), channel_id=1, source_target_pairs={{0,16},{16,0},{1,17},{17,1},{2,18},{18,2},{3,19},{19,3},{4,20},{20... | collective-permute-start | bytes 958472 | tf_op jit(solution)/shard_map/ppermute | solution.py:461
  101.3 31.4 %all-to-all-start.1 = ((bf16[8,64,768]{2,1,0:T(8,128)(2,1)}), bf16[8,64,768]{2,1,0:T(8,128)(2,1)S(1)}, u32[]{:S(2)}, u32[]{:S(2)}) async-start(bf16[8,64,768]{2,1,0:T(8,128)(2,1)} %factor_sum_y.1), calls=%async_computation.1 | async-start | bytes 1572864 | tf_op jit(solution)/shard_map/all_to_all | solution.py:507
  112.0 6.8 %collective-permute-start.14 = (bf16[144,768]{1,0:T(8,128)(2,1)S(1)}, bf16[144,768]{1,0:T(8,128)(2,1)S(1)}, u32[]{:S(2)}, u32[]{:S(2)}) collective-permute-start(bf16[144,768]{1,0:T(8,128)(2,1)S(1)} %get-tuple-element.59), channel_id=1, source_target_pairs={{0,16},{16,0},{1,17},{17,1},{2,18},{18,2},{3,19},{19,3},{4,20},{20... | collective-permute-start | bytes 663560 | tf_op jit(solution)/shard_map/ppermute | solution.py:461
  148.2 10.3 %collective-permute-start.15 = (f32[48,192]{1,0:T(8,128)S(1)}, f32[48,192]{1,0:T(8,128)S(1)}, u32[]{:S(2)}, u32[]{:S(2)}) collective-permute-start(f32[48,192]{1,0:T(8,128)S(1)} %get-tuple-element.62), channel_id=1, source_target_pairs={{0,0},{1,64},{2,128},{3,192},{32,1},{33,65},{34,129},{35,193},{64,... | collective-permute-start | bytes 110600 | tf_op jit(solution)/shard_map/ppermute | solution.py:514
